TPU v7x, 1024 devices: a whole 4x4x32 slice. The times are simulated.
1024 devices in a mesh: grp: 8 (over x, core), clu: 128 (over z, y).
Axes of the slice: x: 4, y: 4, z: 32, core: 2. Of those that a mesh axis runs over, the one named last changes fastest.
Arguments:
- currents: bfloat16 [2, 262144, 128], P(None, ('grp', 'clu')), may hold values from -6 to 6
- live_slots: int32 [262144, 128], P(('grp', 'clu')), may hold values 0 or 1
- radiation: bfloat16 [2, 128, 128], replicated, may hold values from -0.5 to 0.5
- near_tiles: bfloat16 [2, 5, 128, 128], replicated, may hold values from -0.15625 to 0.15625
- leaf_transfer: float32 [2, 31, 128], replicated, may hold values from -1.5 to 1.5
- top_transfer: float32 [2, 31, 512], replicated, may hold values from -0.6 to 0.6
- interpolation: float32 [128, 512], replicated, may hold values from -0.5 to 0.5
- shift_angle: float32 [8, 512], replicated, may hold values from -3.140625 to 3.140625
Outputs:
- field: bfloat16 [2, 262144, 128], P(None, ('grp', 'clu'))
All inputs are finite; a program needn't handle non-finite values. No bound on the sum of `live_slots` on one device may be relied on, other than what follows from the above.
Results may differ from a plain program's by a relative error of at most 0.0034.
The roundings to bfloat16 on the way count: a program that leaves them out, or rounds other values in their place, can miss the bound.
Values may be sent and summed in bfloat16 or wider, within the bound.
No kernel may reach another device: no remote copies, remote signals or barrier semaphores. Data moves between devices by JAX's collectives and lax.ppermute only.
A program may use at most 64 MiB of HBM per device.

v0:
```python
import math

import jax
import jax.numpy as jnp
from jax import lax
from jax.sharding import PartitionSpec as P

K1 = 128
K2 = 512
G = 8
NEAR = 2


def extended_2(cells, sides, width, closed):
    for axis, dim in sides:
        count = lax.axis_size(axis)
        ends = count if closed else count - 1
        head = lax.slice_in_dim(cells, 0, width, axis=dim)
        tail = lax.slice_in_dim(cells, cells.shape[dim] - width, cells.shape[dim], axis=dim)
        cells = jnp.concatenate(
            [
                lax.ppermute(tail, axis, [(i, (i + 1) % count) for i in range(ends)]),
                cells,
                lax.ppermute(head, axis, [((i + 1) % count, i) for i in range(ends)]),
            ],
            axis=dim,
        )
    return cells


def complex_product(left, right):
    return jnp.stack(
        [left[0] * right[0] - left[1] * right[1], left[0] * right[1] + left[1] * right[0]]
    )


def complex_matmul(left, right):
    real_real = jnp.dot(left[0], right[0], preferred_element_type=jnp.float32)
    imag_imag = jnp.dot(left[1], right[1], preferred_element_type=jnp.float32)
    real_imag = jnp.dot(left[0], right[1], preferred_element_type=jnp.float32)
    imag_real = jnp.dot(left[1], right[0], preferred_element_type=jnp.float32)
    return jnp.stack([real_real - imag_imag, real_imag + imag_real])


def complex_receive(left, right):
    dims = (((1,), (1,)), ((), ()))
    real_real = lax.dot_general(left[0], right[0], dims, preferred_element_type=jnp.float32)
    imag_imag = lax.dot_general(left[1], right[1], dims, preferred_element_type=jnp.float32)
    imag_real = lax.dot_general(left[1], right[0], dims, preferred_element_type=jnp.float32)
    real_imag = lax.dot_general(left[0], right[1], dims, preferred_element_type=jnp.float32)
    return jnp.stack([real_real + imag_imag, imag_real - real_imag])


def adjacent(count, offset):
    index = jnp.arange(count, dtype=jnp.int32)
    return jnp.abs(index // G - (index - offset) // G) <= 1


def translated(extended, table, nearest, reach, count, axis):
    result_shape = list(extended.shape)
    result_shape[axis] = count
    total = jnp.zeros(tuple(result_shape), jnp.float32)
    column_shape = [2] + [1] * (extended.ndim - 2) + [table.shape[2]]
    mask_shape = [1] * extended.ndim
    mask_shape[axis] = count
    for offset in range(-reach, reach + 1):
        if abs(offset) < nearest:
            continue
        source = lax.slice_in_dim(extended, reach - offset, reach - offset + count, axis=axis)
        column = table[:, offset + reach].reshape(tuple(column_shape))
        term = complex_product(column, source)
        total = total + jnp.where(adjacent(count, offset).reshape(tuple(mask_shape)), term, 0.0)
    return total


def shards(
    currents,
    live_slots,
    radiation,
    near_tiles,
    leaf_transfer,
    top_transfer,
    interpolation,
    shift_angle,
):
    highest = lax.Precision.HIGHEST
    masked = jnp.where(live_slots[None] == 1, currents, jnp.zeros((), jnp.bfloat16))
    count = currents.shape[1]
    reach = 2 * G - 1
    leaf_patterns = complex_matmul(masked, radiation)
    near_source = extended_2(masked, ((("grp", "clu"), 1),), NEAR, False)
    pattern_source = extended_2(leaf_patterns, ((("grp", "clu"), 1),), reach, False)
    near_field = jnp.zeros(currents.shape, jnp.float32)
    for offset in range(-NEAR, NEAR + 1):
        source = lax.slice_in_dim(near_source, NEAR - offset, NEAR - offset + count, axis=1)
        near_field = near_field + complex_matmul(source, near_tiles[:, offset + NEAR])
    leaf_incoming = translated(pattern_source, leaf_transfer, NEAR + 1, reach, count, 1)
    phase = jnp.stack([jnp.cos(shift_angle), jnp.sin(shift_angle)])
    conjugate = jnp.stack([jnp.cos(shift_angle), -jnp.sin(shift_angle)])
    parents = count // G
    spread = jnp.einsum("snk,km->snm", leaf_patterns, interpolation, precision=highest).reshape(
        2, parents, G, -1
    )
    top_patterns = jnp.sum(complex_product(phase[:, None], spread), axis=2)
    groups = lax.axis_size("grp")
    sliced = top_patterns.shape[2] // groups
    arrived = lax.all_to_all(top_patterns, "grp", split_axis=2, concat_axis=1, tiled=True).reshape(
        2, groups, parents, sliced
    )
    widened_top = extended_2(arrived, (("clu", 2),), reach, True)
    lower = widened_top[:, :, :reach]
    upper = widened_top[:, :, reach + parents :]
    blank = jnp.zeros_like(lower[:, :1])
    position = lax.axis_index("clu")
    lower = jnp.where(position == 0, jnp.concatenate([blank, lower[:, :-1]], axis=1), lower)
    upper = jnp.where(
        position == lax.axis_size("clu") - 1, jnp.concatenate([upper[:, 1:], blank], axis=1), upper
    )
    widened_top = jnp.concatenate(
        [lower, widened_top[:, :, reach : reach + parents], upper], axis=2
    )
    columns = lax.dynamic_slice_in_dim(top_transfer, lax.axis_index("grp") * sliced, sliced, 2)
    local_incoming = translated(widened_top, columns, 2, reach, parents, 2)
    top_incoming = lax.all_to_all(
        local_incoming.reshape(2, groups * parents, sliced),
        "grp",
        split_axis=1,
        concat_axis=2,
        tiled=True,
    )
    spread_back = complex_product(conjugate[:, None], top_incoming[:, :, None, :]).reshape(
        2, count, -1
    )
    returned = jnp.einsum("snm,km->snk", spread_back, interpolation, precision=highest) * math.sqrt(
        K1 / K2
    )
    incoming = (leaf_incoming + returned).astype(jnp.bfloat16)
    far_field = complex_receive(incoming, radiation)
    total = near_field + far_field
    return jnp.where(live_slots[None] == 1, total, 0.0).astype(jnp.bfloat16)


def solution(mesh):
    in_specs = (
        P(None, ("grp", "clu"), None),
        P(("grp", "clu"), None),
        P(),
        P(),
        P(),
        P(),
        P(),
        P(),
    )
    out_specs = P(None, ("grp", "clu"), None)
    return jax.shard_map(shards, mesh=mesh, in_specs=in_specs, out_specs=out_specs, check_vma=False)
```

profile of v0, /device:TPU:1, one launch (start us, length us, event | category | flops | bytes accessed | tf_op | source)
XLA Modules:
  0.0 134.4 jit_solution(9582681047840641112)
XLA Ops:
  0.0 1.0 broadcast_compare_fusion
  1.0 0.8 copy-done.2
  3.1 1.0 fusion.25
  4.8 1.2 reshape.2435
  6.0 17.6 %all-to-all-start = ((f32[8,1,4096]{2,1,0:T(1,128)}), f32[8,1,4096]{2,1,0:T(1,128)S(1)}, u32[]{:S(2)}, u32[]{:S(2)}) async-start(f32[8,1,4096]{2,1,0:T(1,128)} %reshape.2435), calls=%async_computation | async-start | bytes 262144 | tf_op jit(solution)/shard_map/all_to_all | solution.py:107
  23.5 9.1 %collective-permute-start.2 = (f32[2,15,128]{2,1,0:T(8,128)S(1)}, f32[2,15,128]{2,1,0:T(8,128)S(1)}, u32[]{:S(2)}, u32[]{:S(2)}) collective-permute-start(f32[2,15,128]{2,1,0:T(8,128)S(1)} %get-tuple-element.185), channel_id=1, source_target_pairs={{1,0},{2,1},{3,2},{4,3},{5,4},{6,5},{7,6},{8,7},{9,8},{10,9},{11,1... | collective-permute-start | bytes 46088 | tf_op jit(solution)/shard_map/ppermute | solution.py:24
  32.6 1.9 %collective-permute-start.3 = (f32[2,15,128]{2,1,0:T(8,128)S(1)}, f32[2,15,128]{2,1,0:T(8,128)S(1)}, u32[]{:S(2)}, u32[]{:S(2)}) collective-permute-start(f32[2,15,128]{2,1,0:T(8,128)S(1)} %get-tuple-element.186), channel_id=1, source_target_pairs={{0,1},{1,2},{2,3},{3,4},{4,5},{5,6},{6,7},{7,8},{8,9},{9,10},{10,1... | collective-permute-start | bytes 46088 | tf_op jit(solution)/shard_map/ppermute | solution.py:22
  34.6 7.0 %collective-permute-start = (bf16[2,2,128]{2,1,0:T(2,128)(2,1)S(1)}, bf16[2,2,128]{2,1,0:T(2,128)(2,1)S(1)}, u32[]{:S(2)}, u32[]{:S(2)}) collective-permute-start(bf16[2,2,128]{2,1,0:T(2,128)(2,1)S(1)} %get-tuple-element.194), channel_id=1, source_target_pairs={{1,0},{2,1},{3,2},{4,3},{5,4},{6,5},{7,6},{8,7},{9,8},{10,9},{11,1... | collective-permute-start | bytes 3080 | tf_op jit(solution)/shard_map/ppermute | solution.py:24
  41.6 1.9 %collective-permute-start.1 = (bf16[2,2,128]{2,1,0:T(2,128)(2,1)S(1)}, bf16[2,2,128]{2,1,0:T(2,128)(2,1)S(1)}, u32[]{:S(2)}, u32[]{:S(2)}) collective-permute-start(bf16[2,2,128]{2,1,0:T(2,128)(2,1)S(1)} %get-tuple-element.193), channel_id=1, source_target_pairs={{0,1},{1,2},{2,3},{3,4},{4,5},{5,6},{6,7},{7,8},{8,9},{9,10},{10,1... | collective-permute-start | bytes 3080 | tf_op jit(solution)/shard_map/ppermute | solution.py:22
  43.7 0.6 neg.3
  44.4 0.6 slice_bitcast_fusion.69
  46.1 0.6 abs_compare_fusion.2
  46.7 0.6 abs_compare_fusion.4
  47.3 0.6 abs_compare_fusion.6
  50.2 0.6 abs_compare_fusion.16
  50.8 0.6 abs_compare_fusion.18
  53.4 0.7 broadcast_in_dim.504
  54.1 0.6 broadcast_in_dim.508
  54.7 0.7 broadcast_in_dim.511
  55.4 0.6 broadcast_in_dim.514
  56.0 0.7 broadcast_in_dim.517
  57.3 0.6 broadcast_in_dim.523
  57.9 0.7 broadcast_in_dim.526
  58.6 0.7 broadcast_in_dim.529
  59.2 0.7 broadcast_in_dim.532
  59.9 0.7 broadcast_in_dim.535
  60.6 0.6 broadcast_in_dim.538
  61.2 0.6 broadcast_in_dim.541
  61.8 0.6 broadcast_in_dim.544
  62.4 0.6 broadcast_in_dim.547
  63.1 0.6 broadcast_in_dim.550
  63.7 0.7 broadcast_in_dim.553
  64.4 0.7 broadcast_in_dim.556
  65.6 0.6 broadcast_in_dim.562
  66.2 0.6 broadcast_in_dim.565
  67.2 1.7 %fusion.237 = (f32[64]{0:T(128)}, f32[64]{0:T(128)}, f32[64]{0:T(128)}, f32[64]{0:T(128)}, f32[64]{0:T(128)}, /*index=5*/f32[64]{0:T(128)}, f32[64]{0:T(128)}, f...) fusion(f32[2,31,512]{2,0,1:T(2,128)} %param.13, ...), kind=kLoop, calls=%fused_computation.834 | loop fusion | bytes 10288 | tf_op jit(solution)/shard_map/mul | solution.py:33
  68.8 1.9 %fusion.232 = (f32[64]{0:T(128)}, f32[64]{0:T(128)}, f32[64]{0:T(128)}, f32[64]{0:T(128)}, f32[64]{0:T(128)}, /*index=5*/f32[64]{0:T(128)}, f32[64]{0:T(128)}, f...) fusion(f32[2,31,512]{2,0,1:T(2,128)} %param.13, ...), kind=kLoop, calls=%fused_computation.829 | loop fusion | bytes 18504 | tf_op jit(solution)/shard_map/mul | solution.py:33
  71.3 0.6 broadcast_in_dim.571
  72.0 0.6 broadcast_in_dim.574
  72.6 0.7 broadcast_in_dim.577
  73.3 0.7 broadcast_in_dim.580
  74.0 0.6 broadcast_in_dim.583
  74.6 0.6 broadcast_in_dim.586
  77.7 0.8 multiply_subtract_fusion.40
  78.5 1.0 multiply_subtract_fusion.39
  79.5 1.0 multiply_subtract_fusion.38
  80.5 1.0 multiply_subtract_fusion.54
  81.6 1.0 multiply_subtract_fusion.53
  82.5 1.0 multiply_subtract_fusion.52
  83.5 0.9 multiply_subtract_fusion.41
  85.0 0.9 reduce
  86.6 8.9 %collective-permute-start.4 = (f32[2,8,15,64]{3,1,2,0:T(8,128)S(1)}, f32[2,8,15,64]{3,1,2,0:T(8,128)S(1)}, u32[]{:S(2)}, u32[]{:S(2)}) collective-permute-start(f32[2,8,15,64]{3,1,2,0:T(8,128)S(1)} %get-tuple-element.189), channel_id=1, source_target_pairs={{1,0},{2,1},{3,2},{4,3},{5,4},{6,5},{7,6},{8,7},{9,8},{10,9},{11,1... | collective-permute-start | bytes 184328 | tf_op jit(solution)/shard_map/ppermute | solution.py:24
  96.2 1.0 multiply_subtract_fusion.51
  97.2 2.1 %collective-permute-start.5 = (f32[2,8,15,64]{3,1,2,0:T(8,128)S(1)}, f32[2,8,15,64]{3,1,2,0:T(8,128)S(1)}, u32[]{:S(2)}, u32[]{:S(2)}) collective-permute-start(f32[2,8,15,64]{3,1,2,0:T(8,128)S(1)} %get-tuple-element.190), channel_id=1, source_target_pairs={{0,1},{1,2},{2,3},{3,4},{4,5},{5,6},{6,7},{7,8},{8,9},{9,10},{10,1... | collective-permute-start | bytes 184328 | tf_op jit(solution)/shard_map/ppermute | solution.py:22
  104.2 2.2 %collective-permute-done.5 = f32[2,8,15,64]{3,1,2,0:T(8,128)S(1)} collective-permute-done((f32[2,8,15,64]{3,1,2,0:T(8,128)S(1)}, f32[2,8,15,64]{3,1,2,0:T(8,128)S(1)}, u32[]{:S(2)}, u32[]{:S(2)}) %collective-permute-start.5) | collective-permute-done | bytes 61472 | tf_op jit(solution)/shard_map/ppermute | solution.py:22
  112.2 1.8 %fusion.80 = f32[2,256,64]{2,1,0:T(8,128)S(1)} fusion(f32[1,256,64]{2,1,0:T(8,128)S(1)} %bitcast.528, f32[1,256,64]{2,1,0:T(8,128)S(1)} %bitcast.527, f32[1,256,64]{2,1,0:T(8,128)S(1)} %bitcast.520, f32[1,256,64]{2,1,0:T(8,128)S(1)} %bitcast.519, f32[1,256,64]{2,1,0:T(8,128)S(1)} %bitcast.522, f32[1,256,64]{2,1,0:T(8,128)S(1)} %bitcast.521, ...), kind=kLoop, calls=%fused_computation.265 | loop fusion | flops 2719744 | bytes 3808256 | tf_op jit(solution)/shard_map/add | solution.py:72
  114.2 0.9 reshape.2437
  115.1 4.9 %all-to-all-start.1 = ((f32[8,1,4096]{2,1,0:T(1,128)}), f32[8,1,4096]{2,1,0:T(1,128)S(1)}, u32[]{:S(2)}, u32[]{:S(2)}) async-start(f32[8,1,4096]{2,1,0:T(1,128)} %reshape.2437), calls=%async_computation.1 | async-start | bytes 262144 | tf_op jit(solution)/shard_map/all_to_all | solution.py:124
  120.1 0.6 copy-done.61
  120.8 0.8 multiply_subtract_fusion.37
  121.6 3.8 %all-to-all-done.1 = f32[8,1,4096]{2,1,0:T(1,128)S(1)} async-done(((f32[8,1,4096]{2,1,0:T(1,128)}), f32[8,1,4096]{2,1,0:T(1,128)S(1)}, u32[]{:S(2)}, u32[]{:S(2)}) %all-to-all-start.1) | async-done | bytes 131104 | tf_op jit(solution)/shard_map/all_to_all | solution.py:124
  125.3 0.9 reduce.1
  128.8 4.1 %fusion.1 = bf16[2,256,128]{2,1,0:T(8,128)(2,1)S(1)} fusion(f32[1,256,512]{2,1,0:T(8,128)S(1)} %get-tuple-element.192, f32[1,256,512]{2,1,0:T(8,128)S(1)} %get-tuple-element.191, f32[1,256,128]{2,1,0:T(8,128)} %get-tuple-element.167, f32[1,256,128]{2,1,0:T(8,128)} %get-tuple-element.168, f32[128,512]{1,0:T(8,128)S(1)} %copy-done, ...), kind=kOutput, calls=%fused_computation.110 | convolution fusion | flops 408158208 | bytes 8264192 | tf_op jit(solution)/shard_map/snm,km->snk/dot_general | solution.py:134
  133.6 0.7 fusion.24
  (457 shorter events, 26.5 us)
Async XLA Ops:
  0.0 3.1 %copy-start = (f32[128,512]{1,0:T(8,128)S(1)}, f32[128,512]{1,0:T(8,128)}, u32[]{:S(2)}) copy-start(f32[128,512]{1,0:T(8,128)} %param.14) | copy-start | bytes 786436
  0.0 1.0 copy-start.3
  1.0 0.8 copy-start.2
  2.3 0.7 copy-start.24
  6.0 47.1 %copy-start.1 = (bf16[2,5,128,128]{3,2,1,0:T(8,128)(2,1)S(1)}, bf16[2,5,128,128]{3,2,1,0:T(8,128)(2,1)}, u32[]{:S(2)}) copy-start(bf16[2,5,128,128]{3,2,1,0:T(8,128)(2,1)} %param.11) | copy-start | bytes 983044
  6.0 78.5 %all-to-all-start = ((f32[8,1,4096]{2,1,0:T(1,128)}), f32[8,1,4096]{2,1,0:T(1,128)S(1)}, u32[]{:S(2)}, u32[]{:S(2)}) async-start(f32[8,1,4096]{2,1,0:T(1,128)} %reshape.2435), calls=%async_computation | async-start | bytes 262144 | tf_op jit(solution)/shard_map/all_to_all | solution.py:107
  23.5 54.1 %collective-permute-start.2 = (f32[2,15,128]{2,1,0:T(8,128)S(1)}, f32[2,15,128]{2,1,0:T(8,128)S(1)}, u32[]{:S(2)}, u32[]{:S(2)}) collective-permute-start(f32[2,15,128]{2,1,0:T(8,128)S(1)} %get-tuple-element.185), channel_id=1, source_target_pairs={{1,0},{2,1},{3,2},{4,3},{5,4},{6,5},{7,6},{8,7},{9,8},{10,9},{11,1... | collective-permute-start | bytes 46088 | tf_op jit(solution)/shard_map/ppermute | solution.py:24
  32.6 45.0 %collective-permute-start.3 = (f32[2,15,128]{2,1,0:T(8,128)S(1)}, f32[2,15,128]{2,1,0:T(8,128)S(1)}, u32[]{:S(2)}, u32[]{:S(2)}) collective-permute-start(f32[2,15,128]{2,1,0:T(8,128)S(1)} %get-tuple-element.186), channel_id=1, source_target_pairs={{0,1},{1,2},{2,3},{3,4},{4,5},{5,6},{6,7},{7,8},{8,9},{9,10},{10,1... | collective-permute-start | bytes 46088 | tf_op jit(solution)/shard_map/ppermute | solution.py:22
  34.6 9.8 %copy-start.23 = (f32[2,31,128]{2,0,1:T(2,128)S(1)}, f32[2,31,128]{2,0,1:T(2,128)}, u32[]{:S(2)}) copy-start(f32[2,31,128]{2,0,1:T(2,128)} %param.12) | copy-start | bytes 95236
  34.6 40.6 %collective-permute-start = (bf16[2,2,128]{2,1,0:T(2,128)(2,1)S(1)}, bf16[2,2,128]{2,1,0:T(2,128)(2,1)S(1)}, u32[]{:S(2)}, u32[]{:S(2)}) collective-permute-start(bf16[2,2,128]{2,1,0:T(2,128)(2,1)S(1)} %get-tuple-element.194), channel_id=1, source_target_pairs={{1,0},{2,1},{3,2},{4,3},{5,4},{6,5},{7,6},{8,7},{9,8},{10,9},{11,1... | collective-permute-start | bytes 3080 | tf_op jit(solution)/shard_map/ppermute | solution.py:24
  41.6 33.9 %collective-permute-start.1 = (bf16[2,2,128]{2,1,0:T(2,128)(2,1)S(1)}, bf16[2,2,128]{2,1,0:T(2,128)(2,1)S(1)}, u32[]{:S(2)}, u32[]{:S(2)}) collective-permute-start(bf16[2,2,128]{2,1,0:T(2,128)(2,1)S(1)} %get-tuple-element.193), channel_id=1, source_target_pairs={{0,1},{1,2},{2,3},{3,4},{4,5},{5,6},{6,7},{7,8},{8,9},{9,10},{10,1... | collective-permute-start | bytes 3080 | tf_op jit(solution)/shard_map/ppermute | solution.py:22
  86.6 12.7 %collective-permute-start.4 = (f32[2,8,15,64]{3,1,2,0:T(8,128)S(1)}, f32[2,8,15,64]{3,1,2,0:T(8,128)S(1)}, u32[]{:S(2)}, u32[]{:S(2)}) collective-permute-start(f32[2,8,15,64]{3,1,2,0:T(8,128)S(1)} %get-tuple-element.189), channel_id=1, source_target_pairs={{1,0},{2,1},{3,2},{4,3},{5,4},{6,5},{7,6},{8,7},{9,8},{10,9},{11,1... | collective-permute-start | bytes 184328 | tf_op jit(solution)/shard_map/ppermute | solution.py:24
  97.2 9.2 %collective-permute-start.5 = (f32[2,8,15,64]{3,1,2,0:T(8,128)S(1)}, f32[2,8,15,64]{3,1,2,0:T(8,128)S(1)}, u32[]{:S(2)}, u32[]{:S(2)}) collective-permute-start(f32[2,8,15,64]{3,1,2,0:T(8,128)S(1)} %get-tuple-element.190), channel_id=1, source_target_pairs={{0,1},{1,2},{2,3},{3,4},{4,5},{5,6},{6,7},{7,8},{8,9},{9,10},{10,1... | collective-permute-start | bytes 184328 | tf_op jit(solution)/shard_map/ppermute | solution.py:22
  99.3 0.7 copy-start.58
  100.8 0.7 copy-start.82
  102.4 0.7 copy-start.32
  107.4 0.7 copy-start.46
  109.4 0.7 copy-start.25
  111.4 0.7 copy-start.115
  111.5 0.7 copy-start.91
  114.2 5.9 %copy-start.64 = (f32[128]{0:T(128)S(1)}, f32[128]{0:T(128)}, u32[]{:S(2)}) copy-start(f32[128]{0:T(128)} %get-tuple-element.295) | copy-start | bytes 1540
  115.1 10.2 %all-to-all-start.1 = ((f32[8,1,4096]{2,1,0:T(1,128)}), f32[8,1,4096]{2,1,0:T(1,128)S(1)}, u32[]{:S(2)}, u32[]{:S(2)}) async-start(f32[8,1,4096]{2,1,0:T(1,128)} %reshape.2437), calls=%async_computation.1 | async-start | bytes 262144 | tf_op jit(solution)/shard_map/all_to_all | solution.py:124
  120.1 0.7 copy-start.62
  120.1 0.7 copy-start.63
  126.4 1.3 copy-start.21
  126.5 1.3 copy-start.19
  126.5 1.3 copy-start.20
  126.6 0.8 copy-start.22
  126.6 1.2 copy-start.17
  126.6 1.2 copy-start.18
  126.7 1.1 copy-start.15
  126.7 1.1 copy-start.16
  126.8 1.0 copy-start.14
  127.3 1.0 copy-start.5
  127.3 1.0 copy-start.6
  127.4 1.1 copy-start.7
  127.4 1.1 copy-start.8
  127.4 1.1 copy-start.9
  127.4 1.2 copy-start.10
  127.4 1.2 copy-start.11
  127.4 1.2 copy-start.12
  127.4 1.2 copy-start.13
  127.4 1.2 copy-start.122
  127.4 1.2 copy-start.123
  127.4 1.2 copy-start.124
  127.4 1.2 copy-start.125
  127.4 1.2 copy-start.126
  127.5 1.2 copy-start.127
  127.5 1.2 copy-start.128
  127.5 1.2 copy-start.129
  127.5 1.2 copy-start.130
  127.5 1.2 copy-start.131
  127.5 1.2 copy-start.132
  127.5 1.2 copy-start.133
  127.5 1.2 copy-start.134
  127.5 1.2 copy-start.135
  127.5 1.2 copy-start.136
  127.6 1.2 copy-start.137
  127.6 1.2 copy-start.138
  127.6 1.2 copy-start.139
  127.7 1.1 copy-start.4
  127.7 1.1 copy-start.119
  127.8 1.1 copy-start.120
  127.8 1.1 copy-start.121
  (84 other events, 54.2 us)
where the time goes:
time: 135 us; the launch traced here: 134 us
  starting transfers between devices  53.3 us (39%)
  local copies, waits for them, and re-layouts  39.8 us (29%)
  other arithmetic  23.7 us (18%)
  matrix products  9.21 us (7%)
  waiting for transfers between devices  5.93 us (4%)
  between operations  2.32 us (2%)
    ppermute x3, starting transfers between devices, extended_2(): lax.ppermute(head, axis, [((i + 1) % count, i) for i in range(ends)])  24.9 us
    broadcast_in_dim x56, local copies, waits for them, and re-layouts, translated(): jnp.where(adjacent(count, offset).reshape(tuple(mask_shape)), term, 0.0)  17.9 us
    all_to_all x1, starting transfers between devices, shards(): lax.all_to_all(top_patterns, 'grp', split_axis=2, concat_axis=1, tiled=True)  17.6 us
    unnamed x284, local copies, waits for them, and re-layouts  14 us
    sub x21, other arithmetic, complex_product(): left[0] * right[0] - left[1] * right[1]  9.79 us
    le x27, other arithmetic, adjacent(): return jnp.abs(index // G - (index - offset) // G) <= 1  7.73 us
    ppermute x3, starting transfers between devices, extended_2(): lax.ppermute(tail, axis, [(i, (i + 1) % count) for i in range(ends)])  5.93 us
    all_to_all x1, starting transfers between devices, shards(): lax.all_to_all(local_incoming.reshape(2, groups * parents, sliced), 'grp'...  4.92 us
  transfers between devices with their start and end apart: 8, of which 2 were waited for; matrix products, arithmetic and copies ran while one was open for 33% of the time, Pallas kernels for 0%

commit v1 on v0

v1 whole, which is shorter than its diff:
```python
import math

import jax
import jax.numpy as jnp
from jax import lax
from jax.experimental import pallas as pl
from jax.experimental.pallas import tpu as pltpu
from jax.sharding import PartitionSpec as P

G = 8
NEAR = 2
REACH = 2 * G - 1
HALO = G * G
F32 = jnp.float32
BF16 = jnp.bfloat16


def split(values):
    high = values.astype(BF16)
    return high, (values - high.astype(F32)).astype(BF16)


def paired(real, imag):
    return jnp.concatenate(
        [jnp.concatenate([real, imag], axis=1), jnp.concatenate([-imag, real], axis=1)], axis=0
    )


def mm(left, right):
    return jnp.dot(left, right, preferred_element_type=F32)


def mm_t(left, right):
    return lax.dot_general(left, right, (((1,), (1,)), ((), ())), preferred_element_type=F32)


def fill_table(table, transfer, nearest):
    width = transfer.shape[2]
    child = lax.broadcasted_iota(jnp.int32, (G, width), 0)
    for offset in range(-REACH, REACH + 1):
        if abs(offset) < nearest:
            continue
        index = offset + REACH
        real = jnp.broadcast_to(transfer[0, index : index + 1, :], (G, width))
        imag = jnp.broadcast_to(transfer[1, index : index + 1, :], (G, width))
        if offset > G:
            keep = child >= offset - G
        elif offset < -G:
            keep = child <= offset + REACH
        else:
            keep = None
        for part, value in enumerate((real, real + imag, imag - real)):
            table[index, part] = value if keep is None else jnp.where(keep, value, 0.0)


def translated(table, patterns, nearest, start, rows, lanes):
    sums = [jnp.zeros((rows // G, G, lanes.size), F32) for _ in range(3)]
    for offset in range(-REACH, REACH + 1):
        if abs(offset) < nearest:
            continue
        for part in range(3):
            source = patterns[part, pl.ds(start - offset, rows), lanes]
            factor = table[offset + REACH, part, :, lanes]
            sums[part] += factor[None] * source.reshape(rows // G, G, lanes.size)
    real = (sums[0] - sums[1]).reshape(rows, lanes.size)
    imag = (sums[0] + sums[2]).reshape(rows, lanes.size)
    return real, imag


def kernel(
    currents,
    live,
    lower,
    upper,
    radiation,
    tiles,
    leaf_transfer,
    top_transfer,
    interpolation,
    angle,
    field,
    x,
    leaf_table,
    top_table,
    leaf_pat,
    top_pat,
    top_in,
    spread_high,
    spread_low,
    incoming,
):
    count = currents.shape[1]
    k1 = radiation.shape[2]
    k2 = interpolation.shape[1]
    parents = count // G
    wide = parents + 2 * G
    keep = live[...] == 1
    for part in range(2):
        x[part, 0:HALO, :] = lower[part].astype(F32)
        x[part, HALO : HALO + count, :] = jnp.where(keep, currents[part].astype(F32), 0.0)
        x[part, HALO + count :, :] = upper[part].astype(F32)

    def cells(rows):
        return jnp.concatenate([x[0, rows, :], x[1, rows, :]], axis=1).astype(BF16)

    fill_table(leaf_table, leaf_transfer, NEAR + 1)
    fill_table(top_table, top_transfer, 2)
    matrix = paired(radiation[0], radiation[1])
    int_high, int_low = split(interpolation[...])
    cosine = jnp.cos(angle[...])
    sine = jnp.sin(angle[...])

    edge = 2 * G
    natural = mm(cells(pl.ds(HALO - edge, count + 2 * edge)), matrix)
    leaf_pat[0] = natural[:, :k1] + natural[:, k1:]
    leaf_pat[1] = natural[:, k1:]
    leaf_pat[2] = natural[:, :k1]

    ordered = jnp.concatenate([cells(pl.ds(c, wide, stride=G)) for c in range(G)], axis=0)
    by_child = mm(ordered, matrix)
    stacked = jnp.concatenate([by_child[:, :k1], by_child[:, k1:]], axis=0)
    high, low = split(stacked)
    both = jnp.concatenate([high, low], axis=1)
    twice = jnp.concatenate([int_high, int_high], axis=0)
    step = 256
    for begin in range(0, k2, step):
        cols = slice(begin, begin + step)
        spread = mm(both, twice[:, cols]) + mm(high, int_low[:, cols])
        real = jnp.zeros((wide, step), F32)
        imag = jnp.zeros((wide, step), F32)
        for c in range(G):
            sr = spread[c * wide : (c + 1) * wide]
            si = spread[(G + c) * wide : (G + c + 1) * wide]
            cc = cosine[c : c + 1, cols]
            ss = sine[c : c + 1, cols]
            real += cc * sr - ss * si
            imag += cc * si + ss * sr
        top_pat[0, G : G + wide, cols] = real + imag
        top_pat[1, G : G + wide, cols] = imag
        top_pat[2, G : G + wide, cols] = real
    for part in range(3):
        top_pat[part, 0:G, :] = jnp.zeros((G, k2), F32)
        top_pat[part, G + wide :, :] = jnp.zeros((G, k2), F32)

    for begin in range(0, k2, k1):
        lanes = pl.ds(begin, k1)
        real, imag = translated(top_table, top_pat, 2, 2 * G, parents, lanes)
        top_in[0, :, lanes] = real
        top_in[1, :, lanes] = imag

    block = 4 * G
    for begin in range(0, count, block):
        real, imag = translated(leaf_table, leaf_pat, NEAR + 1, edge + begin, block, pl.ds(0, k1))
        incoming[0, begin : begin + block, :] = real
        incoming[1, begin : begin + block, :] = imag

    for pair in range(0, parents, 2):
        reals, imags = [], []
        for p in (pair, pair + 1):
            tr = jnp.broadcast_to(top_in[0, p : p + 1, :], (G, k2))
            ti = jnp.broadcast_to(top_in[1, p : p + 1, :], (G, k2))
            reals.append(cosine * tr + sine * ti)
            imags.append(cosine * ti - sine * tr)
        for part, values in ((0, reals), (1, imags)):
            high, low = split(jnp.concatenate(values, axis=0))
            rows = pl.ds(part * count + pair * G, 2 * G)
            spread_high[rows, :] = high
            spread_low[rows, :] = low
    wide_back = mm_t(spread_high[...], jnp.concatenate([int_high, int_low], axis=0))
    back = wide_back[:, :k1] + wide_back[:, k1:] + mm_t(spread_low[...], int_high)
    back = back * math.sqrt(k1 / k2)
    gathered = jnp.concatenate(
        [
            (incoming[0] + back[:count]).astype(BF16),
            (incoming[1] + back[count:]).astype(BF16),
        ],
        axis=1,
    )
    total = mm_t(gathered, matrix)
    for offset in range(-NEAR, NEAR + 1):
        source = cells(pl.ds(HALO - offset, count))
        total += mm(source, paired(tiles[0, offset + NEAR], tiles[1, offset + NEAR]))
    field[0] = jnp.where(keep, total[:, :k1], 0.0).astype(BF16)
    field[1] = jnp.where(keep, total[:, k1:], 0.0).astype(BF16)


def shards(
    currents,
    live_slots,
    radiation,
    near_tiles,
    leaf_transfer,
    top_transfer,
    interpolation,
    shift_angle,
):
    count = currents.shape[1]
    k1 = radiation.shape[2]
    k2 = interpolation.shape[1]
    axis = ("grp", "clu")
    devices = lax.axis_size(axis)

    def edge(begin):
        cells = lax.slice_in_dim(currents, begin, begin + HALO, axis=1)
        alive = lax.slice_in_dim(live_slots, begin, begin + HALO, axis=0)
        return jnp.where(alive[None] == 1, cells, jnp.zeros((), BF16))

    lower = lax.ppermute(edge(count - HALO), axis, [(i, i + 1) for i in range(devices - 1)])
    upper = lax.ppermute(edge(0), axis, [(i + 1, i) for i in range(devices - 1)])
    wide = count // G + 2 * G
    offsets = 2 * REACH + 1
    return pl.pallas_call(
        kernel,
        out_shape=jax.ShapeDtypeStruct(currents.shape, BF16),
        scratch_shapes=[
            pltpu.VMEM((2, count + 2 * HALO, k1), F32),
            pltpu.VMEM((offsets, 3, G, k1), F32),
            pltpu.VMEM((offsets, 3, G, k2), F32),
            pltpu.VMEM((3, count + 4 * G, k1), F32),
            pltpu.VMEM((3, wide + 2 * G, k2), F32),
            pltpu.VMEM((2, count // G, k2), F32),
            pltpu.VMEM((2 * count, k2), BF16),
            pltpu.VMEM((2 * count, k2), BF16),
            pltpu.VMEM((2, count, k1), F32),
        ],
        compiler_params=pltpu.CompilerParams(vmem_limit_bytes=40 * 1024 * 1024),
        name="fmm",
    )(
        currents,
        live_slots,
        lower,
        upper,
        radiation,
        near_tiles,
        leaf_transfer,
        top_transfer,
        interpolation,
        shift_angle,
    )


def solution(mesh):
    in_specs = (
        P(None, ("grp", "clu"), None),
        P(("grp", "clu"), None),
        P(),
        P(),
        P(),
        P(),
        P(),
        P(),
    )
    out_specs = P(None, ("grp", "clu"), None)
    return jax.shard_map(shards, mesh=mesh, in_specs=in_specs, out_specs=out_specs, check_vma=False)
```

time: 135 us -> 38.8 us (0.29)
  local copies, waits for them, and re-layouts: 39.8 us -> 3.59 us
  starting transfers between devices: 53.3 us -> 24.1 us
  other arithmetic: 23.7 us -> 1.62 us
  matrix products: 9.21 us -> 0 us
  Pallas kernels: 0 us -> 3.84 us
  between operations: 2.32 us -> 0.06 us
    all_to_all x2 -> x0, starting transfers between devices: 22.5 us -> none  [the longest x1 17.6 us: shards(): lax.all_to_all(top_patterns, 'grp', split_axis=2, concat_axis=1, tiled=True)]
    broadcast_in_dim x56 -> x0, local copies, waits for them, and re-layouts: 17.9 us -> none  [translated(): jnp.where(adjacent(count, offset).reshape(tuple(mask_shape)), term, 0.0)]
    unnamed x284 -> x14, local copies, waits for them, and re-layouts: 14 us -> 3.59 us
    sub x21 -> x0, other arithmetic: 9.79 us -> none  [complex_product(): left[0] * right[0] - left[1] * right[1]]
    dot_general x30 -> x0, matrix products: 9.21 us -> none  [the longest x1 4.13 us: shards(): jnp.einsum('snm,km->snk', spread_back, interpolation, precision=highest)]
    le x27 -> x0, other arithmetic: 7.73 us -> none  [adjacent(): return jnp.abs(index // G - (index - offset) // G) <= 1]
    ppermute x6 -> x2, starting transfers between devices: 30.9 us -> 24.1 us  [the longest x1 22.2 us: shards(): lax.ppermute(edge(0), axis, [(i + 1, i) for i in range(devices - 1)])]
    mul x7 -> x0, local copies, waits for them, and re-layouts: 4.93 us -> none  [the longest x5 4.83 us: complex_product(): left[0] * right[0] - left[1] * right[1]]
  transfers between devices with their start and end apart: 8 -> 2, of which waited for: 2 -> 1; matrix products, arithmetic and copies ran while one was open for 33% -> 5% of each run, Pallas kernels for 0% -> 0%
where the time goes in v1:
time: 38.8 us; the launch traced here: 38.4 us
  starting transfers between devices  24.1 us (62%)
  waiting for transfers between devices  5.18 us (13%)
  Pallas kernels  3.84 us (10%)
  local copies, waits for them, and re-layouts  3.59 us (9%)
  other arithmetic  1.62 us (4%)
    ppermute x1, starting transfers between devices, shards(): lax.ppermute(edge(0), axis, [(i + 1, i) for i in range(devices - 1)])  22.2 us
    ppermute x1, waiting for transfers between devices, shards(): lax.ppermute(edge(count - HALO), axis, [(i, i + 1) for i in range(devices...  5.18 us
    pallas_call x1, Pallas kernels, shards(): pl.pallas_call(kernel, out_shape=jax.ShapeDtypeStruct(currents.shape, BF1...  3.84 us
    unnamed x14, local copies, waits for them, and re-layouts  3.59 us
    ppermute x1, starting transfers between devices, shards(): lax.ppermute(edge(count - HALO), axis, [(i, i + 1) for i in range(devices...  1.92 us
    eq x1, other arithmetic, edge(): return jnp.where(alive[None] == 1, cells, jnp.zeros((), BF16))  0.83 us
    select_n x1, other arithmetic, edge(): return jnp.where(alive[None] == 1, cells, jnp.zeros((), BF16))  0.79 us
  transfers between devices with their start and end apart: 2, of which 1 were waited for; matrix products, arithmetic and copies ran while one was open for 5% of the time, Pallas kernels for 0%

profile of v1, /device:TPU:1, one launch (start us, length us, event | category | flops | bytes accessed | tf_op | source)
XLA Modules:
  0.0 38.4 jit_solution(6346561324623869334)
XLA Ops:
  0.0 0.0 copy-start
  0.0 0.8 %slice_compare_fusion = (pred[64,128]{1,0:T(8,128)(4,1)S(1)}, pred[64,128]{1,0:T(8,128)(4,1)S(1)}) fusion(s32[256,128]{1,0:T(8,128)} %live.1), kind=kLoop, calls=%fused_computation.1 | loop fusion | flops 16384 | bytes 81920 | tf_op jit(solution)/shard_map/eq | solution.py:206
  0.8 0.8 %slice_select_fusion = (bf16[2,64,128]{2,1,0:T(8,128)(2,1)S(1)}, bf16[2,64,128]{2,1,0:T(8,128)(2,1)S(1)}) fusion(bf16[2,256,128]{2,1,0:T(8,128)(2,1)} %currents.1, pred[64,128]{1,0:T(8,128)(4,1)S(1)} %get-tuple-element.7, pred[64,128]{1,0:T(8,128)(4,1)S(1)} %get-tuple-element.8), kind=kLoop, calls=%fused_computation | loop fusion | flops 32768 | bytes 147456 | tf_op jit(solution)/shard_map/jit(_where)/select_n | solution.py:206
  1.6 22.2 %collective-permute-start.1 = (bf16[2,64,128]{2,1,0:T(8,128)(2,1)S(1)}, bf16[2,64,128]{2,1,0:T(8,128)(2,1)S(1)}, u32[]{:S(2)}, u32[]{:S(2)}) collective-permute-start(bf16[2,64,128]{2,1,0:T(8,128)(2,1)S(1)} %get-tuple-element.5), channel_id=1, source_target_pairs={{1,0},{2,1},{3,2},{4,3},{5,4},{6,5},{7,6},{8,7},{9,8},{10,9},{11,1... | collective-permute-start | bytes 98312 | tf_op jit(solution)/shard_map/ppermute | solution.py:209
  23.9 1.9 %collective-permute-start = (bf16[2,64,128]{2,1,0:T(8,128)(2,1)S(1)}, bf16[2,64,128]{2,1,0:T(8,128)(2,1)S(1)}, u32[]{:S(2)}, u32[]{:S(2)}) collective-permute-start(bf16[2,64,128]{2,1,0:T(8,128)(2,1)S(1)} %get-tuple-element.6), channel_id=1, source_target_pairs={{0,1},{1,2},{2,3},{3,4},{4,5},{5,6},{6,7},{7,8},{8,9},{9,10},{10,1... | collective-permute-start | bytes 98312 | tf_op jit(solution)/shard_map/ppermute | solution.py:208
  25.8 0.8 %copy.9.leaf_transfer = f32[2,31,128]{2,1,0:T(8,128)S(1)} copy(f32[2,31,128]{2,0,1:T(2,128)} %param.12) | data formatting | bytes 63488 | tf_op args[4]
  26.6 0.0 copy-start.1
  26.6 0.0 copy-start.4
  26.6 0.0 copy-start.5
  26.6 1.0 %copy.10.top_transfer = f32[2,31,512]{2,1,0:T(8,128)S(1)} copy(f32[2,31,512]{2,0,1:T(2,128)} %param.13) | data formatting | bytes 253952 | tf_op args[5]
  27.5 0.0 collective-permute-done.1.upper
  27.5 5.2 %collective-permute-done.lower = bf16[2,64,128]{2,1,0:T(8,128)(2,1)S(1)} collective-permute-done((bf16[2,64,128]{2,1,0:T(8,128)(2,1)S(1)}, bf16[2,64,128]{2,1,0:T(8,128)(2,1)S(1)}, u32[]{:S(2)}, u32[]{:S(2)}) %collective-permute-start) | collective-permute-done | bytes 32800 | tf_op jit(solution)/shard_map/ppermute | solution.py:208
  32.7 0.0 copy-done
  32.7 0.0 copy-done.1
  32.7 0.0 copy-done.4
  32.7 0.0 copy-done.5
  32.7 0.0 copy-start.2
  32.8 0.9 %copy-done.2 = bf16[2,256,128]{2,1,0:T(8,128)(2,1)S(1)} copy-done((bf16[2,256,128]{2,1,0:T(8,128)(2,1)S(1)}, bf16[2,256,128]{2,1,0:T(8,128)(2,1)}, u32[]{:S(2)}) %copy-start.2) | copy-done | bytes 131096
  33.7 0.0 copy-start.3
  33.7 0.9 %copy-done.3 = f32[128,512]{1,0:T(8,128)S(1)} copy-done((f32[128,512]{1,0:T(8,128)S(1)}, f32[128,512]{1,0:T(8,128)}, u32[]{:S(2)}) %copy-start.3) | copy-done | bytes 262168
  34.6 3.8 %fmm.1 = bf16[2,256,128]{2,1,0:T(8,128)(2,1)} custom-call(bf16[2,256,128]{2,1,0:T(8,128)(2,1)S(1)} %copy-done.2, s32[256,128]{1,0:T(8,128)S(1)} %copy-done.1, bf16[2,64,128]{2,1,0:T(8,128)(2,1)S(1)} %collective-permute-done.lower, bf16[2,64,128]{2,1,0:T(8,128)(2,1)S(1)} %collective-permute-done.1.upper, bf16[2,128,128]{2,1,0:T(8,128)(2,1)S(1)} %copy-done.4, ...), custom_call_target="tpu_custom_call" | custom-call | tf_op jit(solution)/shard_map/fmm/pallas_call | solution.py:212
Async XLA Ops:
  0.0 32.7 %copy-start = (bf16[2,5,128,128]{3,2,1,0:T(8,128)(2,1)S(1)}, bf16[2,5,128,128]{3,2,1,0:T(8,128)(2,1)}, u32[]{:S(2)}) copy-start(bf16[2,5,128,128]{3,2,1,0:T(8,128)(2,1)} %tiles.1) | copy-start | bytes 983044
  1.6 25.9 %collective-permute-start.1 = (bf16[2,64,128]{2,1,0:T(8,128)(2,1)S(1)}, bf16[2,64,128]{2,1,0:T(8,128)(2,1)S(1)}, u32[]{:S(2)}, u32[]{:S(2)}) collective-permute-start(bf16[2,64,128]{2,1,0:T(8,128)(2,1)S(1)} %get-tuple-element.5), channel_id=1, source_target_pairs={{1,0},{2,1},{3,2},{4,3},{5,4},{6,5},{7,6},{8,7},{9,8},{10,9},{11,1... | collective-permute-start | bytes 98312 | tf_op jit(solution)/shard_map/ppermute | solution.py:209
  23.9 8.9 %collective-permute-start = (bf16[2,64,128]{2,1,0:T(8,128)(2,1)S(1)}, bf16[2,64,128]{2,1,0:T(8,128)(2,1)S(1)}, u32[]{:S(2)}, u32[]{:S(2)}) collective-permute-start(bf16[2,64,128]{2,1,0:T(8,128)(2,1)S(1)} %get-tuple-element.6), channel_id=1, source_target_pairs={{0,1},{1,2},{2,3},{3,4},{4,5},{5,6},{6,7},{7,8},{8,9},{9,10},{10,1... | collective-permute-start | bytes 98312 | tf_op jit(solution)/shard_map/ppermute | solution.py:208
  26.6 6.2 %copy-start.1 = (s32[256,128]{1,0:T(8,128)S(1)}, s32[256,128]{1,0:T(8,128)}, u32[]{:S(2)}) copy-start(s32[256,128]{1,0:T(8,128)} %live.1) | copy-start | bytes 393220
  26.6 6.2 %copy-start.4 = (bf16[2,128,128]{2,1,0:T(8,128)(2,1)S(1)}, bf16[2,128,128]{2,1,0:T(8,128)(2,1)}, u32[]{:S(2)}) copy-start(bf16[2,128,128]{2,1,0:T(8,128)(2,1)} %radiation.1) | copy-start | bytes 196612
  26.6 6.2 %copy-start.5 = (f32[8,512]{1,0:T(8,128)S(1)}, f32[8,512]{1,0:T(8,128)}, u32[]{:S(2)}) copy-start(f32[8,512]{1,0:T(8,128)} %angle.1) | copy-start | bytes 49156
  32.7 0.9 %copy-start.2 = (bf16[2,256,128]{2,1,0:T(8,128)(2,1)S(1)}, bf16[2,256,128]{2,1,0:T(8,128)(2,1)}, u32[]{:S(2)}) copy-start(bf16[2,256,128]{2,1,0:T(8,128)(2,1)} %currents.1) | copy-start | bytes 393220
  33.7 0.9 %copy-start.3 = (f32[128,512]{1,0:T(8,128)S(1)}, f32[128,512]{1,0:T(8,128)}, u32[]{:S(2)}) copy-start(f32[128,512]{1,0:T(8,128)} %interpolation.1) | copy-start | bytes 786436

commit v2 on v1

v2 whole, which is shorter than its diff:
```python
import math

import jax
import jax.numpy as jnp
from jax import lax
from jax.experimental import pallas as pl
from jax.experimental.pallas import tpu as pltpu
from jax.sharding import PartitionSpec as P

G = 8
NEAR = 2
REACH = 2 * G - 1
HALO = G * G
PAD = 2 * G
F32 = jnp.float32
BF16 = jnp.bfloat16


def split(values):
    high = values.astype(BF16)
    return high, (values - high.astype(F32)).astype(BF16)


def paired(real, imag):
    return jnp.concatenate(
        [jnp.concatenate([real, imag], axis=1), jnp.concatenate([-imag, real], axis=1)], axis=0
    )


def mm(left, right):
    return jnp.dot(left, right, preferred_element_type=F32)


def mm_t(left, right):
    return lax.dot_general(left, right, (((1,), (1,)), ((), ())), preferred_element_type=F32)


def cells(x, rows):
    return jnp.concatenate([x[0, rows, :], x[1, rows, :]], axis=1).astype(BF16)


def fill_table(table, transfer, nearest):
    width = transfer.shape[2]
    child = lax.broadcasted_iota(jnp.int32, (G, width), 0)
    for offset in range(-REACH, REACH + 1):
        if abs(offset) < nearest:
            continue
        index = offset + REACH
        real = jnp.broadcast_to(transfer[index, 0:1, :], (G, width))
        imag = jnp.broadcast_to(transfer[index, 1:2, :], (G, width))
        if offset > G:
            keep = child >= offset - G
        elif offset < -G:
            keep = child <= offset + REACH
        else:
            keep = None
        for part, value in enumerate((real, real + imag, imag - real)):
            table[index, part] = value if keep is None else jnp.where(keep, value, 0.0)


def translated(table, patterns, offsets, start, rows, lanes):
    sums = [jnp.zeros((rows // G, G, lanes.size), F32) for _ in range(3)]
    for offset in offsets:
        for part in range(3):
            source = patterns[part, pl.ds(start - offset, rows), lanes]
            factor = table[offset + REACH, part, :, lanes]
            sums[part] += factor[None] * source.reshape(rows // G, G, lanes.size)
    real = (sums[0] - sums[1]).reshape(rows, lanes.size)
    imag = (sums[0] + sums[2]).reshape(rows, lanes.size)
    return real, imag


def offsets_of(nearest):
    return [d for d in range(-REACH, REACH + 1) if abs(d) >= nearest]


def store_patterns(patterns, rows, lanes, real, imag):
    patterns[0, rows, lanes] = real + imag
    patterns[1, rows, lanes] = imag
    patterns[2, rows, lanes] = real


def aggregated(by_child, parents, weights, cosine, sine, store):
    k1, k2 = weights.shape[0] // 2, weights.shape[1]
    stacked = jnp.concatenate([by_child[:, :k1], by_child[:, k1:]], axis=0)
    high, low = split(stacked)
    both = jnp.concatenate([high, low], axis=1)
    step = 256
    for begin in range(0, k2, step):
        cols = slice(begin, begin + step)
        int_high = weights[:k1, cols]
        twice = jnp.concatenate([int_high, int_high], axis=0)
        spread = mm(both, twice) + mm(high, weights[k1:, cols])
        real = jnp.zeros((parents, step), F32)
        imag = jnp.zeros((parents, step), F32)
        for c in range(G):
            sr = spread[c * parents : (c + 1) * parents]
            si = spread[(G + c) * parents : (G + c + 1) * parents]
            cc = cosine[c : c + 1, cols]
            ss = sine[c : c + 1, cols]
            real += cc * sr - ss * si
            imag += cc * si + ss * sr
        store(cols, real, imag)


def disaggregated(top_in, first, parents, weights, cosine, sine, spread_high, spread_low):
    k1, k2 = weights.shape[0] // 2, weights.shape[1]
    rows_each = parents * G
    for pair in range(0, parents, 2):
        reals, imags = [], []
        for p in (first + pair, first + pair + 1):
            tr = jnp.broadcast_to(top_in[0, p : p + 1, :], (G, k2))
            ti = jnp.broadcast_to(top_in[1, p : p + 1, :], (G, k2))
            reals.append(cosine[...] * tr + sine[...] * ti)
            imags.append(cosine[...] * ti - sine[...] * tr)
        for part, values in ((0, reals), (1, imags)):
            high, low = split(jnp.concatenate(values, axis=0))
            rows = pl.ds(part * rows_each + pair * G, 2 * G)
            spread_high[rows, :] = high
            spread_low[rows, :] = low
    wide = mm_t(spread_high[...], weights[...])
    back = wide[:, :k1] + wide[:, k1:] + mm_t(spread_low[...], weights[:k1])
    back = back * math.sqrt(k1 / k2)
    return back[:rows_each], back[rows_each:]


def local_part(inputs, state, work):
    hbm, staged, sems = inputs
    copies = [pltpu.make_async_copy(a, b, sems.at[i]) for i, (a, b) in enumerate(zip(hbm, staged))]
    for copy in copies:
        copy.start()
    for copy in copies:
        copy.wait()
    currents, live, radiation, tiles, leaf_transfer, top_transfer, interpolation, angle = staged
    (
        middle,
        near_edge,
        leaf_edge,
        top_edge,
        live_edge,
        matrix,
        near,
        weights,
        cosine,
        sine,
        leaf_table,
        top_table,
    ) = state
    x, leaf_pat, top_pat, top_in, spread_high, spread_low, incoming = work
    count = currents.shape[1]
    k1 = radiation.shape[2]
    k2 = interpolation.shape[1]
    parents = count // G
    keep = live[...] == 1
    for part in range(2):
        x[part, 0:PAD, :] = jnp.zeros((PAD, k1), F32)
        x[part, PAD : PAD + count, :] = jnp.where(keep, currents[part].astype(F32), 0.0)
        x[part, PAD + count :, :] = jnp.zeros((PAD, k1), F32)
    live_edge[0:HALO] = live[0:HALO]
    live_edge[HALO:] = live[count - HALO :]
    fill_table(leaf_table, leaf_transfer, NEAR + 1)
    fill_table(top_table, top_transfer, 2)
    matrix[...] = paired(radiation[0], radiation[1])
    for index in range(2 * NEAR + 1):
        near[index] = paired(tiles[0, index], tiles[1, index])
    int_high, int_low = split(interpolation[...])
    weights[:k1] = int_high
    weights[k1:] = int_low
    cosine[...] = jnp.cos(angle[...])
    sine[...] = jnp.sin(angle[...])

    natural = mm(cells(x, pl.ds(0, count + 2 * PAD)), matrix[...])
    store_patterns(leaf_pat, slice(None), slice(None), natural[:, :k1], natural[:, k1:])
    ordered = [cells(x, pl.ds(PAD + c, parents, stride=G)) for c in range(G)]
    by_child = mm(jnp.concatenate(ordered, axis=0), matrix[...])

    def store(cols, real, imag):
        store_patterns(top_pat, pl.ds(PAD, parents), cols, real, imag)

    aggregated(by_child, parents, weights, cosine, sine, store)
    for part in range(3):
        top_pat[part, 0:PAD, :] = jnp.zeros((PAD, k2), F32)
        top_pat[part, PAD + parents :, :] = jnp.zeros((PAD, k2), F32)
    for begin in range(0, k2, k1):
        lanes = pl.ds(begin, k1)
        sums = translated(top_table, top_pat, offsets_of(2), PAD, parents, lanes)
        for part in range(2):
            top_in[part, :, lanes] = sums[part]
            top_edge[part, 0:G, lanes] = sums[part][:G]
            top_edge[part, G:, lanes] = sums[part][parents - G :]
    block = 4 * G
    for begin in range(0, count, block):
        sums = translated(
            leaf_table, leaf_pat, offsets_of(NEAR + 1), PAD + begin, block, pl.ds(0, k1)
        )
        for part in range(2):
            incoming[part, begin : begin + block, :] = sums[part]
    for part in range(2):
        leaf_edge[part, 0:HALO] = incoming[part, 0:HALO]
        leaf_edge[part, HALO:] = incoming[part, count - HALO :]

    total = jnp.zeros((count, 2 * k1), F32)
    for offset in range(-NEAR, NEAR + 1):
        total += mm(cells(x, pl.ds(PAD - offset, count)), near[offset + NEAR])
    near_edge[0:HALO] = total[:HALO]
    near_edge[HALO:] = total[count - HALO :]

    inside = slice(HALO, count - HALO)
    back = disaggregated(
        top_in, G, parents - 2 * G, weights, cosine, sine, spread_high, spread_low
    )
    gathered = jnp.concatenate(
        [(incoming[part, inside] + back[part]).astype(BF16) for part in range(2)], axis=1
    )
    field = mm_t(gathered, matrix[...]) + total[inside]
    for part in range(2):
        values = field[:, part * k1 : (part + 1) * k1]
        middle[part] = jnp.where(keep[inside], values, 0.0).astype(BF16)


def position():
    clu = lax.axis_index("clu")
    leads = jnp.logical_and(clu == 0, lax.axis_index("grp") > 0)
    return lax.rem(clu, 2), jnp.logical_or(leads, clu == 1)


def first_kernel(*refs):
    hbm = refs[:8]
    send_cross, send_inner = refs[8:10]
    state = refs[10:22]
    edge, alive, edge_sems = refs[22:25]
    staged, sems, work = refs[25:33], refs[33], refs[34:]
    currents, live = hbm[:2]
    count = currents.shape[1]
    odd, early = position()
    copies = []
    for side, rows in enumerate((pl.ds(0, HALO), pl.ds(count - HALO, HALO))):
        copies.append(
            pltpu.make_async_copy(currents.at[:, rows, :], edge.at[side], edge_sems.at[side])
        )
        copies.append(
            pltpu.make_async_copy(live.at[rows, :], alive.at[side], edge_sems.at[2 + side])
        )
    for copy in copies:
        copy.start()
    for copy in copies:
        copy.wait()
    for send, side in ((send_cross, odd), (send_inner, 1 - odd)):
        keep = alive[side] == 1
        for part in range(2):
            values = edge[side, part].astype(F32)
            send[part] = jnp.where(keep, values, 0.0).astype(BF16)

    @pl.when(early)
    def _():
        local_part((hbm, staged, sems), state, work)


def last_kernel(*refs):
    hbm = refs[:8]
    received = refs[8:11]
    state = refs[11:23]
    field = refs[23]
    late_state = refs[24:36]
    staged, sems, work = refs[36:44], refs[44], refs[45:52]
    odd, early = position()

    @pl.when(early)
    def _():
        outer_part(received, odd, state, field, refs[52:])

    @pl.when(jnp.logical_not(early))
    def _():
        local_part((hbm, staged, sems), late_state, work)
        outer_part(received, odd, late_state, field, refs[52:])


def outer_part(received, odd, state, field, work):
    (
        middle,
        near_edge,
        leaf_edge,
        top_edge,
        live_edge,
        matrix,
        near,
        weights,
        cosine,
        sine,
        leaf_table,
        top_table,
    ) = state
    cross, inner, inner_late = received
    halo, near_pad, leaf_pad, top_pad, top_sum, edge_high, edge_low, out, out_sems = work
    count = field.shape[1]
    k1 = matrix.shape[0] // 2
    k2 = weights.shape[1]
    inside = pl.ds(HALO, count - 2 * HALO)
    out[:, inside, :] = middle[...]
    middle_copy = pltpu.make_async_copy(
        out.at[:, inside, :], field.at[:, inside, :], out_sems.at[2]
    )
    middle_copy.start()

    for part in range(2):
        halo[part, pl.ds(pl.multiple_of(odd * HALO, HALO), HALO), :] = cross[part].astype(F32)
        halo[part, pl.ds(pl.multiple_of((1 - odd) * HALO, HALO), HALO), :] = inner[part].astype(
            F32
        ) + inner_late[part].astype(F32)
    ordered = [cells(halo, pl.ds(c, 2 * G, stride=G)) for c in range(G)]
    ordered.append(cells(halo, pl.ds(HALO - PAD, 2 * PAD)))
    patterns = mm(jnp.concatenate(ordered, axis=0), matrix[...])

    for part in range(3):
        for side in range(2):
            for begin in (0, 2 * G):
                top_pad[side, part, begin : begin + G, :] = jnp.zeros((G, k2), F32)
                leaf_pad[side, part, begin : begin + G, :] = jnp.zeros((G, k1), F32)

    def store(cols, real, imag):
        for side in range(2):
            rows = slice(side * G, (side + 1) * G)
            store_patterns(top_pad.at[side], pl.ds(G, G), cols, real[rows], imag[rows])

    aggregated(patterns[: 2 * HALO], 2 * G, weights, cosine, sine, store)
    before = lambda nearest: [d for d in offsets_of(nearest) if d > 0]
    after = lambda nearest: [d for d in offsets_of(nearest) if d < 0]
    for side, offsets, start in ((0, before(2), 2 * G), (1, after(2), 0)):
        rows = slice(side * G, (side + 1) * G)
        for begin in range(0, k2, k1):
            lanes = pl.ds(begin, k1)
            sums = translated(top_table, top_pad.at[side], offsets, start, G, lanes)
            for part in range(2):
                top_sum[part, rows, lanes] = top_edge[part, rows, lanes] + sums[part]

    last = 2 * HALO
    leaf_sums = []
    for side, offsets, start in ((0, before(NEAR + 1), 2 * G), (1, after(NEAR + 1), 0)):
        rows = slice(last + G + side * G, last + 2 * G + side * G)
        store_patterns(
            leaf_pad.at[side], pl.ds(G, G), slice(None), patterns[rows, :k1], patterns[rows, k1:]
        )
        leaf_sums.append(
            translated(leaf_table, leaf_pad.at[side], offsets, start, G, pl.ds(0, k1))
        )

    back = disaggregated(top_sum, 0, 2 * G, weights, cosine, sine, edge_high, edge_low)
    parts = []
    for part in range(2):
        blank = jnp.zeros((last - 2 * G, k1), F32)
        extra = jnp.concatenate([leaf_sums[0][part], blank, leaf_sums[1][part]], axis=0)
        parts.append((leaf_edge[part] + extra + back[part]).astype(BF16))
    total = mm_t(jnp.concatenate(parts, axis=1), matrix[...]) + near_edge[...]

    for part in range(2):
        near_pad[0, part] = jnp.zeros((4 * G, k1), F32)
        near_pad[1, part] = jnp.zeros((4 * G, k1), F32)
        near_pad[0, part, G : 2 * G, :] = halo[part, HALO - G : HALO, :]
        near_pad[1, part, 3 * G :, :] = halo[part, HALO : HALO + G, :]
    head = jnp.zeros((PAD, 2 * k1), F32)
    tail = jnp.zeros((PAD, 2 * k1), F32)
    for offset in range(1, NEAR + 1):
        head += mm(cells(near_pad.at[0], pl.ds(2 * G - offset, PAD)), near[NEAR + offset])
        tail += mm(cells(near_pad.at[1], pl.ds(G + offset, PAD)), near[NEAR - offset])
    blank = jnp.zeros((last - 2 * PAD, 2 * k1), F32)
    total = total + jnp.concatenate([head, blank, tail], axis=0)
    keep = live_edge[...] == 1
    for part in range(2):
        values = total[:, part * k1 : (part + 1) * k1]
        values = jnp.where(keep, values, 0.0).astype(BF16)
        out[part, 0:HALO, :] = values[:HALO]
        out[part, count - HALO :, :] = values[HALO:]
    copies = []
    for side, begin in enumerate((0, count - HALO)):
        rows = pl.ds(begin, HALO)
        copies.append(
            pltpu.make_async_copy(
                out.at[:, rows, :], field.at[:, rows, :], out_sems.at[side]
            )
        )
    for copy in copies:
        copy.start()
    for copy in copies:
        copy.wait()
    middle_copy.wait()


def shards(
    currents,
    live_slots,
    radiation,
    near_tiles,
    leaf_transfer,
    top_transfer,
    interpolation,
    shift_angle,
):
    count = currents.shape[1]
    k1 = radiation.shape[2]
    k2 = interpolation.shape[1]
    parents = count // G
    offsets = 2 * REACH + 1
    edge = 2 * HALO
    axis = ("grp", "clu")
    region = lax.axis_size("clu")
    devices = lax.axis_size(axis)
    shape = jax.ShapeDtypeStruct
    hbm = pl.BlockSpec(memory_space=pltpu.HBM)
    vmem = pl.BlockSpec(memory_space=pltpu.VMEM)
    arrays = (
        currents,
        live_slots,
        radiation,
        near_tiles,
        jnp.swapaxes(leaf_transfer, 0, 1),
        jnp.swapaxes(top_transfer, 0, 1),
        interpolation,
        shift_angle,
    )
    arrays = [pltpu.with_memory_space_constraint(a, pltpu.HBM) for a in arrays]
    state = (
        shape((2, count - edge, k1), BF16),
        shape((edge, 2 * k1), F32),
        shape((2, edge, k1), F32),
        shape((2, 2 * G, k2), F32),
        shape((edge, k1), jnp.int32),
        shape((2 * k1, 2 * k1), BF16),
        shape((2 * NEAR + 1, 2 * k1, 2 * k1), BF16),
        shape((2 * k1, k2), BF16),
        shape((G, k2), F32),
        shape((G, k2), F32),
        shape((offsets, 3, G, k1), F32),
        shape((offsets, 3, G, k2), F32),
    )
    local_scratch = [pltpu.VMEM(a.shape, a.dtype) for a in arrays] + [
        pltpu.SemaphoreType.DMA((len(arrays),)),
        pltpu.VMEM((2, count + 2 * PAD, k1), F32),
        pltpu.VMEM((3, count + 2 * PAD, k1), F32),
        pltpu.VMEM((3, parents + 2 * PAD, k2), F32),
        pltpu.VMEM((2, parents, k2), F32),
        pltpu.VMEM((2 * (count - edge), k2), BF16),
        pltpu.VMEM((2 * (count - edge), k2), BF16),
        pltpu.VMEM((2, count, k1), F32),
    ]
    send = shape((2, HALO, k1), BF16)
    params = pltpu.CompilerParams(vmem_limit_bytes=24 * 1024 * 1024)
    send_cross, send_inner, *kept = pl.pallas_call(
        first_kernel,
        out_shape=(send, send) + state,
        in_specs=[hbm] * len(arrays),
        out_specs=(vmem,) * (2 + len(state)),
        scratch_shapes=[
            pltpu.VMEM((2, 2, HALO, k1), BF16),
            pltpu.VMEM((2, HALO, k1), jnp.int32),
            pltpu.SemaphoreType.DMA((4,)),
        ]
        + local_scratch,
        compiler_params=params,
        name="edges_and_early_local",
    )(*arrays)

    def swaps(values, begin, keep):
        pairs = [(i, i + 1) for i in range(begin, devices - 1, 2) if keep(i)]
        return lax.ppermute(values, axis, pairs + [(j, i) for i, j in pairs])

    def leads(i):
        return i > 0 and i % region == 0

    inner = swaps(send_inner, 0, leads)
    send_cross, send_inner, inner = lax.optimization_barrier((send_cross, send_inner, inner))
    cross = swaps(send_cross, 1, lambda i: True)
    inner_late = swaps(send_inner, 0, lambda i: not leads(i))
    return pl.pallas_call(
        last_kernel,
        out_shape=shape(currents.shape, BF16),
        in_specs=[hbm] * len(arrays) + [vmem] * (3 + len(state)),
        out_specs=hbm,
        scratch_shapes=[pltpu.VMEM(a.shape, a.dtype) for a in state]
        + local_scratch
        + [
            pltpu.VMEM((2, edge, k1), F32),
            pltpu.VMEM((2, 2, 4 * G, k1), F32),
            pltpu.VMEM((2, 3, 3 * G, k1), F32),
            pltpu.VMEM((2, 3, 3 * G, k2), F32),
            pltpu.VMEM((2, 2 * G, k2), F32),
            pltpu.VMEM((2 * edge, k2), BF16),
            pltpu.VMEM((2 * edge, k2), BF16),
            pltpu.VMEM((2, count, k1), BF16),
            pltpu.SemaphoreType.DMA((3,)),
        ],
        compiler_params=params,
        name="late_local_and_halo",
    )(*arrays, cross, inner, inner_late, *kept)


def solution(mesh):
    in_specs = (
        P(None, ("grp", "clu"), None),
        P(("grp", "clu"), None),
        P(),
        P(),
        P(),
        P(),
        P(),
        P(),
    )
    out_specs = P(None, ("grp", "clu"), None)
    return jax.shard_map(shards, mesh=mesh, in_specs=in_specs, out_specs=out_specs, check_vma=False)
```

time: 38.8 us -> 27.8 us (0.72)
  starting transfers between devices: 24.1 us -> 18 us
  local copies, waits for them, and re-layouts: 3.59 us -> 0 us
  Pallas kernels: 3.84 us -> 7.26 us
  waiting for transfers between devices: 5.18 us -> 2.2 us
  other arithmetic: 1.62 us -> 0 us
    ppermute x2 -> x3, starting transfers between devices: 24.1 us -> 18 us  [swaps(): return lax.ppermute(values, axis, pairs + [(j, i) for i, j in pairs])]
    unnamed x14 -> x0, local copies, waits for them, and re-layouts: 3.59 us -> none
    pallas_call x1 -> x2, Pallas kernels: 3.84 us -> 7.26 us  [the longest x1 5.17 us: shards(): pl.pallas_call(first_kernel, out_shape=(send, send) + state, in_specs=[hb...]
    ppermute x2 -> x3, waiting for transfers between devices: 5.18 us -> 2.2 us  [swaps(): return lax.ppermute(values, axis, pairs + [(j, i) for i, j in pairs])]
    eq x1 -> x0, other arithmetic: 0.83 us -> none  [edge(): return jnp.where(alive[None] == 1, cells, jnp.zeros((), BF16))]
    select_n x1 -> x0, other arithmetic: 0.79 us -> none  [edge(): return jnp.where(alive[None] == 1, cells, jnp.zeros((), BF16))]
  transfers between devices with their start and end apart: 2 -> 3, of which waited for: 1 -> 2; matrix products, arithmetic and copies ran while one was open for 5% -> 0% of each run, Pallas kernels for 0% -> 0%
where the time goes in v2:
time: 27.8 us; the launch traced here: 27.5 us
  starting transfers between devices  18 us (65%)
  Pallas kernels  7.26 us (26%)
  waiting for transfers between devices  2.2 us (8%)
    ppermute x3, starting transfers between devices, swaps(): return lax.ppermute(values, axis, pairs + [(j, i) for i, j in pairs])  18 us
    pallas_call x1, Pallas kernels, shards(): pl.pallas_call(first_kernel, out_shape=(send, send) + state, in_specs=[hb...  5.17 us
    ppermute x3, waiting for transfers between devices, swaps(): return lax.ppermute(values, axis, pairs + [(j, i) for i, j in pairs])  2.2 us
    pallas_call x1, Pallas kernels, shards(): pl.pallas_call(last_kernel, out_shape=shape(currents.shape, BF16), in_spe...  2.09 us
  transfers between devices with their start and end apart: 3, of which 2 were waited for; matrix products, arithmetic and copies ran while one was open for 0% of the time, Pallas kernels for 0%

profile of v2, /device:TPU:1, one launch (start us, length us, event | category | flops | bytes accessed | tf_op | source)
XLA Modules:
  0.0 27.5 jit_solution(13541831372096456241)
XLA Ops:
  0.0 5.2 %edges_and_early_local.1 = (bf16[2,64,128]{2,1,0:T(8,128)(2,1)S(1)}, bf16[2,64,128]{2,1,0:T(8,128)(2,1)S(1)}, bf16[2,128,128]{2,1,0:T(8,128)(2,1)S(1)}, f32[128,...) custom-call(bf16[2,256,128]{2,1,0:T(8,128)(2,1)} %refs_0_.3, ...), custom_call_target="tpu_custom_call" | custom-call | tf_op jit(solution)/shard_map/edges_and_early_local/pallas_call | solution.py:447
  5.2 4.0 %collective-permute-start = (bf16[2,64,128]{2,1,0:T(8,128)(2,1)S(1)}, bf16[2,64,128]{2,1,0:T(8,128)(2,1)S(1)}, u32[]{:S(2)}, u32[]{:S(2)}) collective-permute-start(bf16[2,64,128]{2,1,0:T(8,128)(2,1)S(1)} %get-tuple-element.26), channel_id=1, source_target_pairs={{128,129},{256,257},{384,385},{512,513},{640,641},{768,769},{896,8... | collective-permute-start | bytes 98312 | tf_op jit(solution)/shard_map/ppermute | solution.py:464
  9.2 1.3 %collective-permute-done.refs_9_ = bf16[2,64,128]{2,1,0:T(8,128)(2,1)S(1)} collective-permute-done((bf16[2,64,128]{2,1,0:T(8,128)(2,1)S(1)}, bf16[2,64,128]{2,1,0:T(8,128)(2,1)S(1)}, u32[]{:S(2)}, u32[]{:S(2)}) %collective-permute-start) | collective-permute-done | bytes 32800 | tf_op jit(solution)/shard_map/ppermute | solution.py:464
  10.5 13.3 %collective-permute-start.1 = (bf16[2,64,128]{2,1,0:T(8,128)(2,1)S(1)}, bf16[2,64,128]{2,1,0:T(8,128)(2,1)S(1)}, u32[]{:S(2)}, u32[]{:S(2)}) collective-permute-start(bf16[2,64,128]{2,1,0:T(8,128)(2,1)S(1)} %get-tuple-element.24), channel_id=1, source_target_pairs={{1,2},{3,4},{5,6},{7,8},{9,10},{11,12},{13,14},{15,16},{17,18},{19... | collective-permute-start | bytes 98312 | tf_op jit(solution)/shard_map/ppermute | solution.py:464
  23.9 0.7 %collective-permute-start.2 = (bf16[2,64,128]{2,1,0:T(8,128)(2,1)S(1)}, bf16[2,64,128]{2,1,0:T(8,128)(2,1)S(1)}, u32[]{:S(2)}, u32[]{:S(2)}) collective-permute-start(bf16[2,64,128]{2,1,0:T(8,128)(2,1)S(1)} %get-tuple-element.26), channel_id=1, source_target_pairs={{0,1},{2,3},{4,5},{6,7},{8,9},{10,11},{12,13},{14,15},{16,17},{18,... | collective-permute-start | bytes 98312 | tf_op jit(solution)/shard_map/ppermute | solution.py:464
  24.5 0.9 %collective-permute-done.1.refs_8_ = bf16[2,64,128]{2,1,0:T(8,128)(2,1)S(1)} collective-permute-done((bf16[2,64,128]{2,1,0:T(8,128)(2,1)S(1)}, bf16[2,64,128]{2,1,0:T(8,128)(2,1)S(1)}, u32[]{:S(2)}, u32[]{:S(2)}) %collective-permute-start.1) | collective-permute-done | bytes 32800 | tf_op jit(solution)/shard_map/ppermute | solution.py:464
  25.4 0.0 collective-permute-done.2.refs_10_
  25.5 2.1 %late_local_and_halo.1 = bf16[2,256,128]{2,1,0:T(8,128)(2,1)} custom-call(bf16[2,256,128]{2,1,0:T(8,128)(2,1)} %refs_0_.3, s32[256,128]{1,0:T(8,128)} %refs_1_.3, bf16[2,128,128]{2,1,0:T(8,128)(2,1)} %refs_2_.3, bf16[2,5,128,128]{3,2,1,0:T(8,128)(2,1)} %refs_3_.3, f32[31,2,128]{2,1,0:T(2,128)} %bitcast.5, f32[31,2,512]{2,1,0:T(2,128)} %bitcast.3, ...), custom_call_target="tpu_custom_call" | custom-call | tf_op jit(solution)/shard_map/late_local_and_halo/pallas_call | solution.py:473
Async XLA Ops:
  5.2 5.3 %collective-permute-start = (bf16[2,64,128]{2,1,0:T(8,128)(2,1)S(1)}, bf16[2,64,128]{2,1,0:T(8,128)(2,1)S(1)}, u32[]{:S(2)}, u32[]{:S(2)}) collective-permute-start(bf16[2,64,128]{2,1,0:T(8,128)(2,1)S(1)} %get-tuple-element.26), channel_id=1, source_target_pairs={{128,129},{256,257},{384,385},{512,513},{640,641},{768,769},{896,8... | collective-permute-start | bytes 98312 | tf_op jit(solution)/shard_map/ppermute | solution.py:464
  10.5 14.9 %collective-permute-start.1 = (bf16[2,64,128]{2,1,0:T(8,128)(2,1)S(1)}, bf16[2,64,128]{2,1,0:T(8,128)(2,1)S(1)}, u32[]{:S(2)}, u32[]{:S(2)}) collective-permute-start(bf16[2,64,128]{2,1,0:T(8,128)(2,1)S(1)} %get-tuple-element.24), channel_id=1, source_target_pairs={{1,2},{3,4},{5,6},{7,8},{9,10},{11,12},{13,14},{15,16},{17,18},{19... | collective-permute-start | bytes 98312 | tf_op jit(solution)/shard_map/ppermute | solution.py:464
  23.9 1.6 %collective-permute-start.2 = (bf16[2,64,128]{2,1,0:T(8,128)(2,1)S(1)}, bf16[2,64,128]{2,1,0:T(8,128)(2,1)S(1)}, u32[]{:S(2)}, u32[]{:S(2)}) collective-permute-start(bf16[2,64,128]{2,1,0:T(8,128)(2,1)S(1)} %get-tuple-element.26), channel_id=1, source_target_pairs={{0,1},{2,3},{4,5},{6,7},{8,9},{10,11},{12,13},{14,15},{16,17},{18,... | collective-permute-start | bytes 98312 | tf_op jit(solution)/shard_map/ppermute | solution.py:464

commit v3 on v2

--- a/solution.py
+++ b/solution.py
@@ -143,6 +143,7 @@
         weights,
         cosine,
         sine,
+        combined,
         leaf_table,
         top_table,
     ) = state
@@ -168,6 +169,11 @@
     weights[k1:] = int_low
     cosine[...] = jnp.cos(angle[...])
     sine[...] = jnp.sin(angle[...])
+    for part in range(2):
+        half = matrix[:, part * k1 : (part + 1) * k1]
+        high, low = split(mm(half, int_high) + mm(half, int_low))
+        combined[0, :, part * k2 : (part + 1) * k2] = high
+        combined[1, :, part * k2 : (part + 1) * k2] = low
 
     natural = mm(cells(x, pl.ds(0, count + 2 * PAD)), matrix[...])
     store_patterns(leaf_pat, slice(None), slice(None), natural[:, :k1], natural[:, k1:])
@@ -221,61 +227,104 @@
 def position():
     clu = lax.axis_index("clu")
     leads = jnp.logical_and(clu == 0, lax.axis_index("grp") > 0)
-    return lax.rem(clu, 2), jnp.logical_or(leads, clu == 1)
-
-
-def first_kernel(*refs):
-    hbm = refs[:8]
-    send_cross, send_inner = refs[8:10]
-    state = refs[10:22]
-    edge, alive, edge_sems = refs[22:25]
-    staged, sems, work = refs[25:33], refs[33], refs[34:]
-    currents, live = hbm[:2]
-    count = currents.shape[1]
-    odd, early = position()
-    copies = []
-    for side, rows in enumerate((pl.ds(0, HALO), pl.ds(count - HALO, HALO))):
-        copies.append(
-            pltpu.make_async_copy(currents.at[:, rows, :], edge.at[side], edge_sems.at[side])
-        )
-        copies.append(
-            pltpu.make_async_copy(live.at[rows, :], alive.at[side], edge_sems.at[2 + side])
-        )
-    for copy in copies:
-        copy.start()
-    for copy in copies:
-        copy.wait()
-    for send, side in ((send_cross, odd), (send_inner, 1 - odd)):
-        keep = alive[side] == 1
-        for part in range(2):
-            values = edge[side, part].astype(F32)
-            send[part] = jnp.where(keep, values, 0.0).astype(BF16)
-
-    @pl.when(early)
+    return lax.rem(clu, 2), leads
+
+
+def lead_kernel(*refs):
+    hbm, send, state = refs[:8], refs[8], refs[9:22]
+    alive, edge_sems = refs[22:24]
+    staged, sems, work = refs[24:32], refs[32], refs[33:]
+    odd, leads = position()
+
+    @pl.when(jnp.logical_and(lax.axis_index("clu") < 2, lax.axis_index("grp") > 0))
+    def _():
+        currents, live = hbm[:2]
+        begin = (1 - odd) * (currents.shape[1] - HALO)
+        rows = pl.ds(pl.multiple_of(begin, HALO), HALO)
+        copies = [
+            pltpu.make_async_copy(currents.at[:, rows, :], send, edge_sems.at[0]),
+            pltpu.make_async_copy(live.at[rows, :], alive, edge_sems.at[1]),
+        ]
+        for copy in copies:
+            copy.start()
+        for copy in copies:
+            copy.wait()
+        mask(send, send, alive[...])
+
+    @pl.when(leads)
     def _():
         local_part((hbm, staged, sems), state, work)
 
 
+def mask(target, source, alive):
+    for part in range(2):
+        target[part] = jnp.where(alive == 1, source[part].astype(F32), 0.0).astype(BF16)
+
+
+def edge_kernel(currents, live, after, cross, inner):
+    odd, _ = position()
+    begin = currents.shape[1] - HALO
+    for target, side in ((cross, odd), (inner, 1 - odd)):
+        rows = pl.ds(pl.multiple_of(side * begin, HALO), HALO)
+        mask(target, currents.at[:, rows, :], live[rows, :])
+
+
+def inner_kernel(*refs):
+    inner, state, rows = refs[0], refs[1:14], refs[16]
+    halo, *work = refs[17:]
+    odd, leads = position()
+
+    @pl.when(leads)
+    def _():
+        for part in range(2):
+            halo[part, HALO:, :] = inner[part].astype(F32)
+        outer_part(halo, (1,), state, (rows,), work)
+
+
 def last_kernel(*refs):
     hbm = refs[:8]
-    received = refs[8:11]
-    state = refs[11:23]
-    field = refs[23]
-    late_state = refs[24:36]
-    staged, sems, work = refs[36:44], refs[44], refs[45:52]
-    odd, early = position()
-
-    @pl.when(early)
+    cross, inner, inner_late, inner_rows = refs[8:12]
+    state = refs[12:25]
+    field = refs[25]
+    late_state = refs[26:39]
+    staged, sems, local_work = refs[39:47], refs[47], refs[48:55]
+    lower, upper, out_sems, halo, *work = refs[55:]
+    count = field.shape[1]
+    inside = pl.ds(HALO, count - 2 * HALO)
+    head, tail = pl.ds(0, HALO), pl.ds(count - HALO, HALO)
+    odd, leads = position()
+
+    def sent(source, rows, index):
+        copy = pltpu.make_async_copy(source, field.at[:, rows, :], out_sems.at[index])
+        copy.start()
+        return copy
+
+    @pl.when(leads)
     def _():
-        outer_part(received, odd, state, field, refs[52:])
-
-    @pl.when(jnp.logical_not(early))
+        copies = [sent(state[0], inside, 0), sent(inner_rows, tail, 1)]
+        for part in range(2):
+            halo[part, 0:HALO, :] = cross[part].astype(F32)
+        outer_part(halo, (0,), state, (lower,), work)
+        copies.append(sent(lower, head, 2))
+        for copy in copies:
+            copy.wait()
+
+    @pl.when(jnp.logical_not(leads))
     def _():
-        local_part((hbm, staged, sems), late_state, work)
-        outer_part(received, odd, late_state, field, refs[52:])
-
-
-def outer_part(received, odd, state, field, work):
+        local_part((hbm, staged, sems), late_state, local_work)
+        copies = [sent(late_state[0], inside, 0)]
+        for part in range(2):
+            halo[part, pl.ds(pl.multiple_of(odd * HALO, HALO), HALO), :] = cross[part].astype(F32)
+            halo[part, pl.ds(pl.multiple_of((1 - odd) * HALO, HALO), HALO), :] = inner[
+                part
+            ].astype(F32) + inner_late[part].astype(F32)
+        outer_part(halo, (0, 1), late_state, (lower, upper), work)
+        copies += [sent(upper, tail, 1), sent(lower, head, 2)]
+        for copy in copies:
+            copy.wait()
+
+
+def outer_part(halo, sides, state, fields, work):
     (
         middle,
         near_edge,
@@ -287,102 +336,123 @@
         weights,
         cosine,
         sine,
+        combined,
         leaf_table,
         top_table,
     ) = state
-    cross, inner, inner_late = received
-    halo, near_pad, leaf_pad, top_pad, top_sum, edge_high, edge_low, out, out_sems = work
-    count = field.shape[1]
+    near_pad, leaf_pad, top_pad, top_sum, edge_high, edge_low = work
     k1 = matrix.shape[0] // 2
     k2 = weights.shape[1]
-    inside = pl.ds(HALO, count - 2 * HALO)
-    out[:, inside, :] = middle[...]
-    middle_copy = pltpu.make_async_copy(
-        out.at[:, inside, :], field.at[:, inside, :], out_sems.at[2]
-    )
-    middle_copy.start()
-
-    for part in range(2):
-        halo[part, pl.ds(pl.multiple_of(odd * HALO, HALO), HALO), :] = cross[part].astype(F32)
-        halo[part, pl.ds(pl.multiple_of((1 - odd) * HALO, HALO), HALO), :] = inner[part].astype(
-            F32
-        ) + inner_late[part].astype(F32)
-    ordered = [cells(halo, pl.ds(c, 2 * G, stride=G)) for c in range(G)]
-    ordered.append(cells(halo, pl.ds(HALO - PAD, 2 * PAD)))
-    patterns = mm(jnp.concatenate(ordered, axis=0), matrix[...])
-
+    rows_of = [slice(side * HALO, (side + 1) * HALO) for side in sides]
+    wide = len(sides) * G
+
+    def both(rows):
+        return jnp.concatenate([halo[0, rows, :], halo[1, rows, :]], axis=1)
+
+    ordered = [both(pl.ds(side * HALO + c, G, stride=G)) for c in range(G) for side in sides]
+    ordered = jnp.concatenate(ordered, axis=0).astype(BF16)
     for part in range(3):
-        for side in range(2):
+        for side in sides:
             for begin in (0, 2 * G):
                 top_pad[side, part, begin : begin + G, :] = jnp.zeros((G, k2), F32)
                 leaf_pad[side, part, begin : begin + G, :] = jnp.zeros((G, k1), F32)
-
-    def store(cols, real, imag):
-        for side in range(2):
-            rows = slice(side * G, (side + 1) * G)
+    step = 256
+    for begin in range(0, k2, step):
+        cols = slice(begin, begin + step)
+        spread = []
+        for first in (begin, k2 + begin):
+            taken = slice(first, first + step)
+            spread.append(mm(ordered, combined[0, :, taken]) + mm(ordered, combined[1, :, taken]))
+        real = jnp.zeros((wide, step), F32)
+        imag = jnp.zeros((wide, step), F32)
+        for c in range(G):
+            sr, si = [value[c * wide : (c + 1) * wide] for value in spread]
+            cc = cosine[c : c + 1, cols]
+            ss = sine[c : c + 1, cols]
+            real += cc * sr - ss * si
+            imag += cc * si + ss * sr
+        for at, side in enumerate(sides):
+            rows = slice(at * G, (at + 1) * G)
             store_patterns(top_pad.at[side], pl.ds(G, G), cols, real[rows], imag[rows])
 
-    aggregated(patterns[: 2 * HALO], 2 * G, weights, cosine, sine, store)
-    before = lambda nearest: [d for d in offsets_of(nearest) if d > 0]
-    after = lambda nearest: [d for d in offsets_of(nearest) if d < 0]
-    for side, offsets, start in ((0, before(2), 2 * G), (1, after(2), 0)):
-        rows = slice(side * G, (side + 1) * G)
+    def reaching(side, nearest):
+        return [d for d in offsets_of(nearest) if (d > 0) == (side == 0)]
+
+    starts = (2 * G, 0)
+    for at, side in enumerate(sides):
         for begin in range(0, k2, k1):
             lanes = pl.ds(begin, k1)
-            sums = translated(top_table, top_pad.at[side], offsets, start, G, lanes)
+            sums = translated(
+                top_table, top_pad.at[side], reaching(side, 2), starts[side], G, lanes
+            )
             for part in range(2):
-                top_sum[part, rows, lanes] = top_edge[part, rows, lanes] + sums[part]
-
-    last = 2 * HALO
+                known = top_edge[part, side * G : (side + 1) * G, lanes]
+                top_sum[part, at * G : (at + 1) * G, lanes] = known + sums[part]
+
     leaf_sums = []
-    for side, offsets, start in ((0, before(NEAR + 1), 2 * G), (1, after(NEAR + 1), 0)):
-        rows = slice(last + G + side * G, last + 2 * G + side * G)
+    for side in sides:
+        window = both(pl.ds(HALO - PAD if side == 0 else HALO, PAD)).astype(BF16)
+        patterns = mm(window, matrix[...])
+        rows = slice(G, 2 * G) if side == 0 else slice(0, G)
         store_patterns(
             leaf_pad.at[side], pl.ds(G, G), slice(None), patterns[rows, :k1], patterns[rows, k1:]
         )
         leaf_sums.append(
-            translated(leaf_table, leaf_pad.at[side], offsets, start, G, pl.ds(0, k1))
-        )
-
-    back = disaggregated(top_sum, 0, 2 * G, weights, cosine, sine, edge_high, edge_low)
-    parts = []
-    for part in range(2):
-        blank = jnp.zeros((last - 2 * G, k1), F32)
-        extra = jnp.concatenate([leaf_sums[0][part], blank, leaf_sums[1][part]], axis=0)
-        parts.append((leaf_edge[part] + extra + back[part]).astype(BF16))
-    total = mm_t(jnp.concatenate(parts, axis=1), matrix[...]) + near_edge[...]
-
-    for part in range(2):
-        near_pad[0, part] = jnp.zeros((4 * G, k1), F32)
-        near_pad[1, part] = jnp.zeros((4 * G, k1), F32)
-        near_pad[0, part, G : 2 * G, :] = halo[part, HALO - G : HALO, :]
-        near_pad[1, part, 3 * G :, :] = halo[part, HALO : HALO + G, :]
-    head = jnp.zeros((PAD, 2 * k1), F32)
-    tail = jnp.zeros((PAD, 2 * k1), F32)
-    for offset in range(1, NEAR + 1):
-        head += mm(cells(near_pad.at[0], pl.ds(2 * G - offset, PAD)), near[NEAR + offset])
-        tail += mm(cells(near_pad.at[1], pl.ds(G + offset, PAD)), near[NEAR - offset])
-    blank = jnp.zeros((last - 2 * PAD, 2 * k1), F32)
-    total = total + jnp.concatenate([head, blank, tail], axis=0)
-    keep = live_edge[...] == 1
-    for part in range(2):
-        values = total[:, part * k1 : (part + 1) * k1]
-        values = jnp.where(keep, values, 0.0).astype(BF16)
-        out[part, 0:HALO, :] = values[:HALO]
-        out[part, count - HALO :, :] = values[HALO:]
-    copies = []
-    for side, begin in enumerate((0, count - HALO)):
-        rows = pl.ds(begin, HALO)
-        copies.append(
-            pltpu.make_async_copy(
-                out.at[:, rows, :], field.at[:, rows, :], out_sems.at[side]
+            translated(
+                leaf_table,
+                leaf_pad.at[side],
+                reaching(side, NEAR + 1),
+                starts[side],
+                G,
+                pl.ds(0, k1),
             )
         )
-    for copy in copies:
-        copy.start()
-    for copy in copies:
-        copy.wait()
-    middle_copy.wait()
+
+    near_sums = []
+    for side in sides:
+        for part in range(2):
+            near_pad[side, part] = jnp.zeros((4 * G, k1), F32)
+            if side == 0:
+                near_pad[0, part, G : 2 * G, :] = halo[part, HALO - G : HALO, :]
+            else:
+                near_pad[1, part, 3 * G :, :] = halo[part, HALO : HALO + G, :]
+        total = jnp.zeros((PAD, 2 * k1), F32)
+        for offset in range(1, NEAR + 1):
+            start = 2 * G - offset if side == 0 else G + offset
+            signed = offset if side == 0 else -offset
+            total += mm(cells(near_pad.at[side], pl.ds(start, PAD)), near[NEAR + signed])
+        near_sums.append(total)
+
+    size = len(sides) * HALO
+    back = disaggregated(
+        top_sum,
+        0,
+        wide,
+        weights,
+        cosine,
+        sine,
+        edge_high.at[0 : 2 * size],
+        edge_low.at[0 : 2 * size],
+    )
+    for at, side in enumerate(sides):
+        blank = jnp.zeros((HALO - G, k1), F32)
+        parts = []
+        for part in range(2):
+            extra = [leaf_sums[at][part], blank]
+            extra = jnp.concatenate(extra if side == 0 else extra[::-1], axis=0)
+            known = leaf_edge[part, rows_of[at], :]
+            parts.append(
+                (known + extra + back[part][at * HALO : (at + 1) * HALO]).astype(BF16)
+            )
+        blank = jnp.zeros((HALO - PAD, 2 * k1), F32)
+        extra = [near_sums[at], blank]
+        extra = jnp.concatenate(extra if side == 0 else extra[::-1], axis=0)
+        total = mm_t(jnp.concatenate(parts, axis=1), matrix[...])
+        total = total + near_edge[rows_of[at], :] + extra
+        keep = live_edge[rows_of[at], :] == 1
+        for part in range(2):
+            values = total[:, part * k1 : (part + 1) * k1]
+            fields[at][part] = jnp.where(keep, values, 0.0).astype(BF16)
 
 
 def shards(
@@ -429,6 +499,7 @@
         shape((2 * k1, k2), BF16),
         shape((G, k2), F32),
         shape((G, k2), F32),
+        shape((2, 2 * k1, 2 * k2), BF16),
         shape((offsets, 3, G, k1), F32),
         shape((offsets, 3, G, k2), F32),
     )
@@ -444,53 +515,69 @@
     ]
     send = shape((2, HALO, k1), BF16)
     params = pltpu.CompilerParams(vmem_limit_bytes=24 * 1024 * 1024)
-    send_cross, send_inner, *kept = pl.pallas_call(
-        first_kernel,
-        out_shape=(send, send) + state,
+    send_lead, *kept = pl.pallas_call(
+        lead_kernel,
+        out_shape=(send,) + state,
         in_specs=[hbm] * len(arrays),
-        out_specs=(vmem,) * (2 + len(state)),
-        scratch_shapes=[
-            pltpu.VMEM((2, 2, HALO, k1), BF16),
-            pltpu.VMEM((2, HALO, k1), jnp.int32),
-            pltpu.SemaphoreType.DMA((4,)),
-        ]
+        out_specs=(vmem,) * (1 + len(state)),
+        scratch_shapes=[pltpu.VMEM((HALO, k1), jnp.int32), pltpu.SemaphoreType.DMA((2,))]
         + local_scratch,
         compiler_params=params,
-        name="edges_and_early_local",
+        cost_estimate=pl.CostEstimate(flops=10**9, bytes_accessed=4*10**6, transcendentals=8192),
+        name="lead_local",
     )(*arrays)
 
     def swaps(values, begin, keep):
         pairs = [(i, i + 1) for i in range(begin, devices - 1, 2) if keep(i)]
         return lax.ppermute(values, axis, pairs + [(j, i) for i, j in pairs])
 
-    def leads(i):
+    def leading(i):
         return i > 0 and i % region == 0
 
-    inner = swaps(send_inner, 0, leads)
-    send_cross, send_inner, inner = lax.optimization_barrier((send_cross, send_inner, inner))
+    inner = swaps(send_lead, 0, leading)
+    outer_scratch = [
+        pltpu.VMEM((2, edge, k1), F32),
+        pltpu.VMEM((2, 2, 4 * G, k1), F32),
+        pltpu.VMEM((2, 3, 3 * G, k1), F32),
+        pltpu.VMEM((2, 3, 3 * G, k2), F32),
+        pltpu.VMEM((2, 2 * G, k2), F32),
+        pltpu.VMEM((2 * edge, k2), BF16),
+        pltpu.VMEM((2 * edge, k2), BF16),
+    ]
+    near_cells = [pltpu.with_memory_space_constraint(a, pltpu.VMEM) for a in (currents, live_slots)]
+    inner_rows = pl.pallas_call(
+        inner_kernel,
+        out_shape=send,
+        in_specs=[vmem] * (3 + len(state)),
+        out_specs=vmem,
+        scratch_shapes=outer_scratch,
+        compiler_params=params,
+        cost_estimate=pl.CostEstimate(flops=0, bytes_accessed=0, transcendentals=0),
+        name="inner_side",
+    )(inner, *kept, *near_cells)
+    send_cross, send_inner = pl.pallas_call(
+        edge_kernel,
+        out_shape=(send, send),
+        in_specs=[vmem] * 3,
+        out_specs=(vmem,) * 2,
+        compiler_params=params,
+        name="edges",
+    )(*near_cells, inner_rows)
     cross = swaps(send_cross, 1, lambda i: True)
-    inner_late = swaps(send_inner, 0, lambda i: not leads(i))
+    inner_late = swaps(send_inner, 0, lambda i: not leading(i))
     return pl.pallas_call(
         last_kernel,
         out_shape=shape(currents.shape, BF16),
-        in_specs=[hbm] * len(arrays) + [vmem] * (3 + len(state)),
+        in_specs=[hbm] * len(arrays) + [vmem] * (4 + len(state)),
         out_specs=hbm,
         scratch_shapes=[pltpu.VMEM(a.shape, a.dtype) for a in state]
         + local_scratch
-        + [
-            pltpu.VMEM((2, edge, k1), F32),
-            pltpu.VMEM((2, 2, 4 * G, k1), F32),
-            pltpu.VMEM((2, 3, 3 * G, k1), F32),
-            pltpu.VMEM((2, 3, 3 * G, k2), F32),
-            pltpu.VMEM((2, 2 * G, k2), F32),
-            pltpu.VMEM((2 * edge, k2), BF16),
-            pltpu.VMEM((2 * edge, k2), BF16),
-            pltpu.VMEM((2, count, k1), BF16),
-            pltpu.SemaphoreType.DMA((3,)),
-        ],
+        + [pltpu.VMEM(send.shape, BF16)] * 2
+        + [pltpu.SemaphoreType.DMA((3,))]
+        + outer_scratch,
         compiler_params=params,
         name="late_local_and_halo",
-    )(*arrays, cross, inner, inner_late, *kept)
+    )(*arrays, cross, inner, inner_late, inner_rows, *kept)
 
 
 def solution(mesh):

time: 27.8 us -> 26.5 us (0.953)
  starting transfers between devices: 18 us -> 14.9 us
  waiting for transfers between devices: 2.2 us -> 3.65 us
  Pallas kernels: 7.26 us -> 7.75 us
    ppermute x3, starting transfers between devices: 18 us -> 14.9 us  [swaps(): return lax.ppermute(values, axis, pairs + [(j, i) for i, j in pairs])]
    ppermute x3, waiting for transfers between devices: 2.2 us -> 3.65 us  [swaps(): return lax.ppermute(values, axis, pairs + [(j, i) for i, j in pairs])]
    pallas_call x1 -> x3, Pallas kernels: 5.17 us -> 6.22 us  [the longest x1 5.44 us: shards(): pl.pallas_call(lead_kernel, out_shape=(send,) + state, in_specs=[hbm] * l...]
    pallas_call x1, Pallas kernels: 2.09 us -> 1.53 us  [shards(): pl.pallas_call(last_kernel, out_shape=shape(currents.shape, BF16), in_spe...]
where the time goes in v3:
time: 26.5 us; the launch traced here: 26.4 us
  starting transfers between devices  14.9 us (56%)
  Pallas kernels  7.75 us (29%)
  waiting for transfers between devices  3.65 us (14%)
    ppermute x3, starting transfers between devices, swaps(): return lax.ppermute(values, axis, pairs + [(j, i) for i, j in pairs])  14.9 us
    pallas_call x1, Pallas kernels, shards(): pl.pallas_call(lead_kernel, out_shape=(send,) + state, in_specs=[hbm] * l...  5.44 us
    ppermute x3, waiting for transfers between devices, swaps(): return lax.ppermute(values, axis, pairs + [(j, i) for i, j in pairs])  3.65 us
    pallas_call x1, Pallas kernels, shards(): pl.pallas_call(last_kernel, out_shape=shape(currents.shape, BF16), in_spe...  1.53 us
    pallas_call x1, Pallas kernels, shards(): pl.pallas_call(inner_kernel, out_shape=send, in_specs=[vmem] * (3 + len(s...  0.75 us
  transfers between devices with their start and end apart: 3, of which 2 were waited for; matrix products, arithmetic and copies ran while one was open for 0% of the time, Pallas kernels for 0%

profile of v3, /device:TPU:1, one launch (start us, length us, event | category | flops | bytes accessed | tf_op | source)
XLA Modules:
  0.0 26.4 jit_solution(1689363473458993384)
XLA Ops:
  0.0 0.0 copy-start
  0.0 0.0 copy-start.1
  0.0 5.4 %lead_local.1 = (bf16[2,64,128]{2,1,0:T(8,128)(2,1)S(1)}, bf16[2,128,128]{2,1,0:T(8,128)(2,1)S(1)}, f32[128,256]{1,0:T(8,128)S(1)}, f32[2,128,128]{2,1,0:T(8,128...) custom-call(bf16[2,256,128]{2,1,0:T(8,128)(2,1)} %refs_0_.3, ...), custom_call_target="tpu_custom_call" | custom-call | flops 1000000000 | bytes 4000000 | tf_op jit(solution)/shard_map/lead_local/pallas_call | solution.py:518
  5.5 1.9 %collective-permute-start = (bf16[2,64,128]{2,1,0:T(8,128)(2,1)S(1)}, bf16[2,64,128]{2,1,0:T(8,128)(2,1)S(1)}, u32[]{:S(2)}, u32[]{:S(2)}) collective-permute-start(bf16[2,64,128]{2,1,0:T(8,128)(2,1)S(1)} %get-tuple-element.21), channel_id=1, source_target_pairs={{128,129},{256,257},{384,385},{512,513},{640,641},{768,769},{896,8... | collective-permute-start | bytes 98312 | tf_op jit(solution)/shard_map/ppermute | solution.py:532
  7.4 2.7 %collective-permute-done.refs_0_.refs_9_ = bf16[2,64,128]{2,1,0:T(8,128)(2,1)S(1)} collective-permute-done((bf16[2,64,128]{2,1,0:T(8,128)(2,1)S(1)}, bf16[2,64,128]{2,1,0:T(8,128)(2,1)S(1)}, u32[]{:S(2)}, u32[]{:S(2)}) %collective-permute-start) | collective-permute-done | bytes 32800 | tf_op jit(solution)/shard_map/ppermute | solution.py:532
  10.1 0.0 copy-done
  10.1 0.0 copy-done.1
  10.1 0.8 %inner_side.1.after.refs_11_ = bf16[2,64,128]{2,1,0:T(8,128)(2,1)S(1)} custom-call(bf16[2,64,128]{2,1,0:T(8,128)(2,1)S(1)} %collective-permute-done.refs_0_.refs_9_, bf16[2,128,128]{2,1,0:T(8,128)(2,1)S(1)} %get-tuple-element.22.refs_1_.refs_12_, f32[128,256]{1,0:T(8,128)S(1)} %get-tuple-element.23.refs_2_.refs_13_, ...), custom_call_target="tpu_custom_call" | custom-call | tf_op jit(solution)/shard_map/inner_side/pallas_call | solution.py:548
  10.9 12.3 %collective-permute-start.1 = (bf16[2,64,128]{2,1,0:T(8,128)(2,1)S(1)}, bf16[2,64,128]{2,1,0:T(8,128)(2,1)S(1)}, u32[]{:S(2)}, u32[]{:S(2)}) collective-permute-start(bf16[2,64,128]{2,1,0:T(8,128)(2,1)S(1)} %get-tuple-element.35), channel_id=1, source_target_pairs={{1,2},{3,4},{5,6},{7,8},{9,10},{11,12},{13,14},{15,16},{17,18},{19... | collective-permute-start | bytes 98312 | tf_op jit(solution)/shard_map/ppermute | solution.py:532
  23.2 0.7 %collective-permute-start.2 = (bf16[2,64,128]{2,1,0:T(8,128)(2,1)S(1)}, bf16[2,64,128]{2,1,0:T(8,128)(2,1)S(1)}, u32[]{:S(2)}, u32[]{:S(2)}) collective-permute-start(bf16[2,64,128]{2,1,0:T(8,128)(2,1)S(1)} %get-tuple-element.36), channel_id=1, source_target_pairs={{0,1},{2,3},{4,5},{6,7},{8,9},{10,11},{12,13},{14,15},{16,17},{18,... | collective-permute-start | bytes 98312 | tf_op jit(solution)/shard_map/ppermute | solution.py:532
  23.9 0.9 %collective-permute-done.1.refs_8_ = bf16[2,64,128]{2,1,0:T(8,128)(2,1)S(1)} collective-permute-done((bf16[2,64,128]{2,1,0:T(8,128)(2,1)S(1)}, bf16[2,64,128]{2,1,0:T(8,128)(2,1)S(1)}, u32[]{:S(2)}, u32[]{:S(2)}) %collective-permute-start.1) | collective-permute-done | bytes 32800 | tf_op jit(solution)/shard_map/ppermute | solution.py:532
  24.8 0.0 collective-permute-done.2.refs_10_
  24.8 1.5 %late_local_and_halo.1 = bf16[2,256,128]{2,1,0:T(8,128)(2,1)} custom-call(bf16[2,256,128]{2,1,0:T(8,128)(2,1)} %refs_0_.3, s32[256,128]{1,0:T(8,128)} %refs_1_.3, bf16[2,128,128]{2,1,0:T(8,128)(2,1)} %refs_2_.3, bf16[2,5,128,128]{3,2,1,0:T(8,128)(2,1)} %refs_3_.3, f32[31,2,128]{2,1,0:T(2,128)} %bitcast.5, f32[31,2,512]{2,1,0:T(2,128)} %bitcast.3, ...), custom_call_target="tpu_custom_call" | custom-call | tf_op jit(solution)/shard_map/late_local_and_halo/pallas_call | solution.py:568
  (1 shorter events, 0.0 us)
Async XLA Ops:
  0.0 10.1 %copy-start = (bf16[2,256,128]{2,1,0:T(8,128)(2,1)S(1)}, bf16[2,256,128]{2,1,0:T(8,128)(2,1)}, u32[]{:S(2)}) copy-start(bf16[2,256,128]{2,1,0:T(8,128)(2,1)} %refs_0_.3) | copy-start | bytes 393220
  0.0 10.1 %copy-start.1 = (s32[256,128]{1,0:T(8,128)S(1)}, s32[256,128]{1,0:T(8,128)}, u32[]{:S(2)}) copy-start(s32[256,128]{1,0:T(8,128)} %refs_1_.3) | copy-start | bytes 393220
  5.5 4.7 %collective-permute-start = (bf16[2,64,128]{2,1,0:T(8,128)(2,1)S(1)}, bf16[2,64,128]{2,1,0:T(8,128)(2,1)S(1)}, u32[]{:S(2)}, u32[]{:S(2)}) collective-permute-start(bf16[2,64,128]{2,1,0:T(8,128)(2,1)S(1)} %get-tuple-element.21), channel_id=1, source_target_pairs={{128,129},{256,257},{384,385},{512,513},{640,641},{768,769},{896,8... | collective-permute-start | bytes 98312 | tf_op jit(solution)/shard_map/ppermute | solution.py:532
  10.9 13.9 %collective-permute-start.1 = (bf16[2,64,128]{2,1,0:T(8,128)(2,1)S(1)}, bf16[2,64,128]{2,1,0:T(8,128)(2,1)S(1)}, u32[]{:S(2)}, u32[]{:S(2)}) collective-permute-start(bf16[2,64,128]{2,1,0:T(8,128)(2,1)S(1)} %get-tuple-element.35), channel_id=1, source_target_pairs={{1,2},{3,4},{5,6},{7,8},{9,10},{11,12},{13,14},{15,16},{17,18},{19... | collective-permute-start | bytes 98312 | tf_op jit(solution)/shard_map/ppermute | solution.py:532
  23.2 1.6 %collective-permute-start.2 = (bf16[2,64,128]{2,1,0:T(8,128)(2,1)S(1)}, bf16[2,64,128]{2,1,0:T(8,128)(2,1)S(1)}, u32[]{:S(2)}, u32[]{:S(2)}) collective-permute-start(bf16[2,64,128]{2,1,0:T(8,128)(2,1)S(1)} %get-tuple-element.36), channel_id=1, source_target_pairs={{0,1},{2,3},{4,5},{6,7},{8,9},{10,11},{12,13},{14,15},{16,17},{18,... | collective-permute-start | bytes 98312 | tf_op jit(solution)/shard_map/ppermute | solution.py:532

commit v4 on v3

--- a/solution.py
+++ b/solution.py
@@ -54,20 +54,20 @@
             keep = child <= offset + REACH
         else:
             keep = None
-        for part, value in enumerate((real, real + imag, imag - real)):
+        for part, value in enumerate((real, imag)):
             table[index, part] = value if keep is None else jnp.where(keep, value, 0.0)
 
 
 def translated(table, patterns, offsets, start, rows, lanes):
-    sums = [jnp.zeros((rows // G, G, lanes.size), F32) for _ in range(3)]
+    tiles = (rows // G, G, lanes.size)
+    real = jnp.zeros(tiles, F32)
+    imag = jnp.zeros(tiles, F32)
     for offset in offsets:
-        for part in range(3):
-            source = patterns[part, pl.ds(start - offset, rows), lanes]
-            factor = table[offset + REACH, part, :, lanes]
-            sums[part] += factor[None] * source.reshape(rows // G, G, lanes.size)
-    real = (sums[0] - sums[1]).reshape(rows, lanes.size)
-    imag = (sums[0] + sums[2]).reshape(rows, lanes.size)
-    return real, imag
+        pr, pi = [patterns[q, pl.ds(start - offset, rows), lanes].reshape(tiles) for q in range(2)]
+        tr, ti = [table[offset + REACH, q, :, lanes][None] for q in range(2)]
+        real += tr * pr - ti * pi
+        imag += tr * pi + ti * pr
+    return real.reshape(rows, lanes.size), imag.reshape(rows, lanes.size)
 
 
 def offsets_of(nearest):
@@ -75,9 +75,8 @@
 
 
 def store_patterns(patterns, rows, lanes, real, imag):
-    patterns[0, rows, lanes] = real + imag
+    patterns[0, rows, lanes] = real
     patterns[1, rows, lanes] = imag
-    patterns[2, rows, lanes] = real
 
 
 def aggregated(by_child, parents, weights, cosine, sine, store):
@@ -184,7 +183,7 @@
         store_patterns(top_pat, pl.ds(PAD, parents), cols, real, imag)
 
     aggregated(by_child, parents, weights, cosine, sine, store)
-    for part in range(3):
+    for part in range(2):
         top_pat[part, 0:PAD, :] = jnp.zeros((PAD, k2), F32)
         top_pat[part, PAD + parents :, :] = jnp.zeros((PAD, k2), F32)
     for begin in range(0, k2, k1):
@@ -351,7 +350,7 @@
 
     ordered = [both(pl.ds(side * HALO + c, G, stride=G)) for c in range(G) for side in sides]
     ordered = jnp.concatenate(ordered, axis=0).astype(BF16)
-    for part in range(3):
+    for part in range(2):
         for side in sides:
             for begin in (0, 2 * G):
                 top_pad[side, part, begin : begin + G, :] = jnp.zeros((G, k2), F32)
@@ -500,14 +499,14 @@
         shape((G, k2), F32),
         shape((G, k2), F32),
         shape((2, 2 * k1, 2 * k2), BF16),
-        shape((offsets, 3, G, k1), F32),
-        shape((offsets, 3, G, k2), F32),
+        shape((offsets, 2, G, k1), F32),
+        shape((offsets, 2, G, k2), F32),
     )
     local_scratch = [pltpu.VMEM(a.shape, a.dtype) for a in arrays] + [
         pltpu.SemaphoreType.DMA((len(arrays),)),
         pltpu.VMEM((2, count + 2 * PAD, k1), F32),
-        pltpu.VMEM((3, count + 2 * PAD, k1), F32),
-        pltpu.VMEM((3, parents + 2 * PAD, k2), F32),
+        pltpu.VMEM((2, count + 2 * PAD, k1), F32),
+        pltpu.VMEM((2, parents + 2 * PAD, k2), F32),
         pltpu.VMEM((2, parents, k2), F32),
         pltpu.VMEM((2 * (count - edge), k2), BF16),
         pltpu.VMEM((2 * (count - edge), k2), BF16),
@@ -538,8 +537,8 @@
     outer_scratch = [
         pltpu.VMEM((2, edge, k1), F32),
         pltpu.VMEM((2, 2, 4 * G, k1), F32),
-        pltpu.VMEM((2, 3, 3 * G, k1), F32),
-        pltpu.VMEM((2, 3, 3 * G, k2), F32),
+        pltpu.VMEM((2, 2, 3 * G, k1), F32),
+        pltpu.VMEM((2, 2, 3 * G, k2), F32),
         pltpu.VMEM((2, 2 * G, k2), F32),
         pltpu.VMEM((2 * edge, k2), BF16),
         pltpu.VMEM((2 * edge, k2), BF16),

time: 26.5 us -> 26.5 us (level)
  no operation moved by 1% of the time
where the time goes in v4:
time: 26.5 us; the launch traced here: 26.3 us
  starting transfers between devices  14.8 us (56%)
  Pallas kernels  7.79 us (29%)
  waiting for transfers between devices  3.65 us (14%)
    ppermute x3, starting transfers between devices, swaps(): return lax.ppermute(values, axis, pairs + [(j, i) for i, j in pairs])  14.8 us
    pallas_call x1, Pallas kernels, shards(): pl.pallas_call(lead_kernel, out_shape=(send,) + state, in_specs=[hbm] * l...  5.54 us
    ppermute x3, waiting for transfers between devices, swaps(): return lax.ppermute(values, axis, pairs + [(j, i) for i, j in pairs])  3.65 us
    pallas_call x1, Pallas kernels, shards(): pl.pallas_call(last_kernel, out_shape=shape(currents.shape, BF16), in_spe...  1.47 us
    pallas_call x1, Pallas kernels, shards(): pl.pallas_call(inner_kernel, out_shape=send, in_specs=[vmem] * (3 + len(s...  0.75 us
  transfers between devices with their start and end apart: 3, of which 2 were waited for; matrix products, arithmetic and copies ran while one was open for 0% of the time, Pallas kernels for 0%

profile of v4, /device:TPU:1, one launch (start us, length us, event | category | flops | bytes accessed | tf_op | source)
XLA Modules:
  0.0 26.3 jit_solution(10341690027330257059)
XLA Ops:
  0.0 0.0 copy-start
  0.0 0.0 copy-start.1
  0.0 5.5 %lead_local.1 = (bf16[2,64,128]{2,1,0:T(8,128)(2,1)S(1)}, bf16[2,128,128]{2,1,0:T(8,128)(2,1)S(1)}, f32[128,256]{1,0:T(8,128)S(1)}, f32[2,128,128]{2,1,0:T(8,128...) custom-call(bf16[2,256,128]{2,1,0:T(8,128)(2,1)} %refs_0_.3, ...), custom_call_target="tpu_custom_call" | custom-call | flops 1000000000 | bytes 4000000 | tf_op jit(solution)/shard_map/lead_local/pallas_call | solution.py:517
  5.6 1.9 %collective-permute-start = (bf16[2,64,128]{2,1,0:T(8,128)(2,1)S(1)}, bf16[2,64,128]{2,1,0:T(8,128)(2,1)S(1)}, u32[]{:S(2)}, u32[]{:S(2)}) collective-permute-start(bf16[2,64,128]{2,1,0:T(8,128)(2,1)S(1)} %get-tuple-element.21), channel_id=1, source_target_pairs={{128,129},{256,257},{384,385},{512,513},{640,641},{768,769},{896,8... | collective-permute-start | bytes 98312 | tf_op jit(solution)/shard_map/ppermute | solution.py:531
  7.5 2.7 %collective-permute-done.refs_0_.refs_9_ = bf16[2,64,128]{2,1,0:T(8,128)(2,1)S(1)} collective-permute-done((bf16[2,64,128]{2,1,0:T(8,128)(2,1)S(1)}, bf16[2,64,128]{2,1,0:T(8,128)(2,1)S(1)}, u32[]{:S(2)}, u32[]{:S(2)}) %collective-permute-start) | collective-permute-done | bytes 32800 | tf_op jit(solution)/shard_map/ppermute | solution.py:531
  10.2 0.0 copy-done
  10.2 0.0 copy-done.1
  10.2 0.7 %inner_side.1.after.refs_11_ = bf16[2,64,128]{2,1,0:T(8,128)(2,1)S(1)} custom-call(bf16[2,64,128]{2,1,0:T(8,128)(2,1)S(1)} %collective-permute-done.refs_0_.refs_9_, bf16[2,128,128]{2,1,0:T(8,128)(2,1)S(1)} %get-tuple-element.22.refs_1_.refs_12_, f32[128,256]{1,0:T(8,128)S(1)} %get-tuple-element.23.refs_2_.refs_13_, ...), custom_call_target="tpu_custom_call" | custom-call | tf_op jit(solution)/shard_map/inner_side/pallas_call | solution.py:547
  11.0 12.2 %collective-permute-start.1 = (bf16[2,64,128]{2,1,0:T(8,128)(2,1)S(1)}, bf16[2,64,128]{2,1,0:T(8,128)(2,1)S(1)}, u32[]{:S(2)}, u32[]{:S(2)}) collective-permute-start(bf16[2,64,128]{2,1,0:T(8,128)(2,1)S(1)} %get-tuple-element.35), channel_id=1, source_target_pairs={{1,2},{3,4},{5,6},{7,8},{9,10},{11,12},{13,14},{15,16},{17,18},{19... | collective-permute-start | bytes 98312 | tf_op jit(solution)/shard_map/ppermute | solution.py:531
  23.2 0.7 %collective-permute-start.2 = (bf16[2,64,128]{2,1,0:T(8,128)(2,1)S(1)}, bf16[2,64,128]{2,1,0:T(8,128)(2,1)S(1)}, u32[]{:S(2)}, u32[]{:S(2)}) collective-permute-start(bf16[2,64,128]{2,1,0:T(8,128)(2,1)S(1)} %get-tuple-element.36), channel_id=1, source_target_pairs={{0,1},{2,3},{4,5},{6,7},{8,9},{10,11},{12,13},{14,15},{16,17},{18,... | collective-permute-start | bytes 98312 | tf_op jit(solution)/shard_map/ppermute | solution.py:531
  23.9 0.9 %collective-permute-done.1.refs_8_ = bf16[2,64,128]{2,1,0:T(8,128)(2,1)S(1)} collective-permute-done((bf16[2,64,128]{2,1,0:T(8,128)(2,1)S(1)}, bf16[2,64,128]{2,1,0:T(8,128)(2,1)S(1)}, u32[]{:S(2)}, u32[]{:S(2)}) %collective-permute-start.1) | collective-permute-done | bytes 32800 | tf_op jit(solution)/shard_map/ppermute | solution.py:531
  24.8 0.0 collective-permute-done.2.refs_10_
  24.8 1.5 %late_local_and_halo.1 = bf16[2,256,128]{2,1,0:T(8,128)(2,1)} custom-call(bf16[2,256,128]{2,1,0:T(8,128)(2,1)} %refs_0_.3, s32[256,128]{1,0:T(8,128)} %refs_1_.3, bf16[2,128,128]{2,1,0:T(8,128)(2,1)} %refs_2_.3, bf16[2,5,128,128]{3,2,1,0:T(8,128)(2,1)} %refs_3_.3, f32[31,2,128]{2,1,0:T(2,128)} %bitcast.5, f32[31,2,512]{2,1,0:T(2,128)} %bitcast.3, ...), custom_call_target="tpu_custom_call" | custom-call | tf_op jit(solution)/shard_map/late_local_and_halo/pallas_call | solution.py:567
  (1 shorter events, 0.0 us)
Async XLA Ops:
  0.0 10.2 %copy-start = (bf16[2,256,128]{2,1,0:T(8,128)(2,1)S(1)}, bf16[2,256,128]{2,1,0:T(8,128)(2,1)}, u32[]{:S(2)}) copy-start(bf16[2,256,128]{2,1,0:T(8,128)(2,1)} %refs_0_.3) | copy-start | bytes 393220
  0.0 10.2 %copy-start.1 = (s32[256,128]{1,0:T(8,128)S(1)}, s32[256,128]{1,0:T(8,128)}, u32[]{:S(2)}) copy-start(s32[256,128]{1,0:T(8,128)} %refs_1_.3) | copy-start | bytes 393220
  5.6 4.7 %collective-permute-start = (bf16[2,64,128]{2,1,0:T(8,128)(2,1)S(1)}, bf16[2,64,128]{2,1,0:T(8,128)(2,1)S(1)}, u32[]{:S(2)}, u32[]{:S(2)}) collective-permute-start(bf16[2,64,128]{2,1,0:T(8,128)(2,1)S(1)} %get-tuple-element.21), channel_id=1, source_target_pairs={{128,129},{256,257},{384,385},{512,513},{640,641},{768,769},{896,8... | collective-permute-start | bytes 98312 | tf_op jit(solution)/shard_map/ppermute | solution.py:531
  11.0 13.8 %collective-permute-start.1 = (bf16[2,64,128]{2,1,0:T(8,128)(2,1)S(1)}, bf16[2,64,128]{2,1,0:T(8,128)(2,1)S(1)}, u32[]{:S(2)}, u32[]{:S(2)}) collective-permute-start(bf16[2,64,128]{2,1,0:T(8,128)(2,1)S(1)} %get-tuple-element.35), channel_id=1, source_target_pairs={{1,2},{3,4},{5,6},{7,8},{9,10},{11,12},{13,14},{15,16},{17,18},{19... | collective-permute-start | bytes 98312 | tf_op jit(solution)/shard_map/ppermute | solution.py:531
  23.2 1.6 %collective-permute-start.2 = (bf16[2,64,128]{2,1,0:T(8,128)(2,1)S(1)}, bf16[2,64,128]{2,1,0:T(8,128)(2,1)S(1)}, u32[]{:S(2)}, u32[]{:S(2)}) collective-permute-start(bf16[2,64,128]{2,1,0:T(8,128)(2,1)S(1)} %get-tuple-element.36), channel_id=1, source_target_pairs={{0,1},{2,3},{4,5},{6,7},{8,9},{10,11},{12,13},{14,15},{16,17},{18,... | collective-permute-start | bytes 98312 | tf_op jit(solution)/shard_map/ppermute | solution.py:531
